TPU v7x, 256 devices: a whole 4x4x8 slice. The times are simulated.
256 devices in a mesh: dp: 32 (over z_hi, x, core), tensor: 8 (over z_lo, y).
Axes of the slice: x: 4, y: 4, z: 8 (z_hi: 4, z_lo: 2; z = z_hi * 2 + z_lo), core: 2. Of those that a mesh axis runs over, the one named last changes fastest.
Arguments:
- activations: bfloat16 [256, 256, 14336], P('dp', None, 'tensor'), may hold values from -6 to 6
- out_grads: bfloat16 [256, 256, 4096], P('dp', None, 'tensor'), may hold values from -6 to 6
- signs_in: int32 [14336], P('tensor'), may hold values from 0 to 1
- signs_out: int32 [4096], P('tensor'), may hold values from 0 to 1
- picks_in: int32 [64], replicated, may hold values from 0 to 14335
- picks_out: int32 [64], replicated, may hold values from 0 to 4095
- test_sketches: bfloat16 [1024, 4096], P('tensor', 'dp'), may hold values from -0.09375 to 0.09375
Outputs:
- scores: float32 [256, 1024], P('dp', 'tensor')
All inputs are finite; a program needn't handle non-finite values.
Results may differ from a plain program's by a relative error of at most 0.0029.
Values may be sent and summed in bfloat16 or wider, within the bound.
No kernel may reach another device: no remote copies, remote signals or barrier semaphores. Data moves between devices by JAX's collectives and lax.ppermute only.
A program may use at most 64 MiB of HBM per device.

v0:
```python
import math

import jax
import jax.numpy as jnp
from jax import lax
from jax.sharding import PartitionSpec as P

HB = 256


def parity_sign(left, right):
    common = jnp.bitwise_and(left, right)
    ones_count = jnp.zeros_like(common)
    for position in range(12):
        ones_count = ones_count + jnp.bitwise_and(jnp.right_shift(common, position), 1)
    return (1 - 2 * jnp.bitwise_and(ones_count, 1)).astype(jnp.float32)


def local_pick(local_width, my_index, sign_bits, chosen):
    offsets = jnp.arange(local_width, dtype=jnp.int32)[:, None]
    target = chosen[None, :]
    matches = offsets // HB == target % local_width // HB
    signed = parity_sign(my_index + jnp.zeros_like(offsets), target // local_width) * parity_sign(
        offsets % HB, target % HB
    )
    flips = (2 * sign_bits - 1).astype(jnp.float32)[:, None]
    return jnp.where(matches, signed * flips, jnp.float32(0.0)).astype(jnp.bfloat16)


def outer_sum(picked_out, picked_in):
    return jnp.einsum("etk,etl->ekl", picked_out, picked_in, precision=lax.Precision.HIGHEST)


def on_device(activations, out_grads, signs_in, signs_out, picks_in, picks_out, test_sketches):
    tp_parts = lax.axis_size("tensor")
    my_index = lax.axis_index("tensor")
    examples, tokens, local_in = activations.shape
    norm_scale = 1.0 / math.sqrt(HB * tp_parts)
    in_matrix = local_pick(local_in, my_index, signs_in, picks_in)
    out_matrix = local_pick(out_grads.shape[2], my_index, signs_out, picks_out)
    term_in = (
        jnp.einsum("etf,fk->etk", activations, in_matrix, preferred_element_type=jnp.float32)
        * norm_scale
    )
    term_out = (
        jnp.einsum("etf,fk->etk", out_grads, out_matrix, preferred_element_type=jnp.float32)
        * norm_scale
    )
    picked_in, picked_out = lax.psum((term_in, term_out), "tensor")
    outer = outer_sum(picked_out, picked_in)
    sketch = (outer / math.sqrt(tokens)).reshape(examples, -1).astype(jnp.bfloat16)
    contract = (((1,), (1,)), ((), ()))
    return lax.dot_general(
        sketch,
        lax.all_gather(test_sketches, "dp", axis=1, tiled=True),
        contract,
        preferred_element_type=jnp.float32,
    )


def solution(mesh):
    in_specs = (
        P("dp", None, "tensor"),
        P("dp", None, "tensor"),
        P("tensor"),
        P("tensor"),
        P(),
        P(),
        P("tensor", "dp"),
    )
    out_specs = P("dp", "tensor")
    return jax.shard_map(
        on_device, mesh=mesh, in_specs=in_specs, out_specs=out_specs, check_vma=False
    )
```

profile of v0, /device:TPU:2, one launch (start us, length us, event | category | flops | bytes accessed | tf_op | source)
XLA Modules:
  0.0 114.9 jit_solution(1097023123037385294)
XLA Ops:
  7.4 0.0 copy-start
  7.4 0.0 all-reduce.3.cloned.1.call-start
  7.4 0.9 add_convert_fusion
  8.2 0.7 add_convert_fusion.1
  8.9 0.7 and_select_fusion.2
  9.6 6.3 %fusion = f32[8,256,64]{1,2,0:T(8,128)} fusion(bf16[8,256,1792]{2,1,0:T(8,128)(2,1)} %param.7, f32[1792]{0:T(1024)S(1)} %add_convert_fusion, s32[64]{0:T(128)S(1)} %get-tuple-element.9, s32[1792]{0:T(1024)S(1)} %get-tuple-element.18, f32[64]{0:T(128)S(1)} %get-tuple-element.8, s32[1792]{0:T(1024)S(1)} %get-tuple-element.19, s32[64]{0:T(128)S(1)} %get-tuple-element.7), kind=kOutput, calls=%fused_computation.13 | convolution fusion | flops 475054080 | bytes 7886592 | tf_op jit(solution)/shard_map/etf,fk->etk/dot_general | solution.py:42
  16.0 0.0 copy-done
  16.0 1.7 %fusion.1 = f32[8,256,64]{1,2,0:T(8,128)} fusion(bf16[8,256,512]{2,1,0:T(8,128)(2,1)S(1)} %copy-done, f32[512]{0:T(512)S(1)} %add_convert_fusion.1, s32[64]{0:T(128)S(1)} %get-tuple-element.13, s32[512]{0:T(512)S(1)} %get-tuple-element.16, f32[64]{0:T(128)S(1)} %get-tuple-element.14, s32[512]{0:T(512)S(1)} %get-tuple-element.17, s32[64]{0:T(128)S(1)} %get-tuple-element.15), kind=kOutput, calls=%fused_computation.15 | convolution fusion | flops 135823360 | bytes 2628352 | tf_op jit(solution)/shard_map/etf,fk->etk/dot_general | solution.py:46
  17.6 0.0 all-reduce.3.cloned.1.call-update
  17.6 0.0 all-gather.2.cloned.1.call-start
  17.7 0.5 all-gather.2.cloned.1.call-update
  18.2 85.0 %all-reduce.3.cloned.1.call-done = (f32[8,256,64]{1,2,0:T(8,128)}, f32[8,256,64]{1,2,0:T(8,128)}) async-done(((f32[8,256,64]{1,2,0:T(8,128)}, f32[8,256,64]{1,2,0:T(8,128)}), (f32[8,256,64]{1,2,0:T(8,128)}, f32[8,256,64]{1,2,0:T(8,128)})) %all-reduce.3.cloned.1.call-update) | async-done | bytes 1048592 | tf_op jit(solution)/shard_map/psum | solution.py:49
  103.2 1.8 %fusion.2 = bf16[8,64,64]{2,1,0:T(8,128)(2,1)S(1)} fusion(f32[8,256,64]{1,2,0:T(8,128)} %get-tuple-element.5, f32[8,256,64]{1,2,0:T(8,128)} %get-tuple-element.6), kind=kOutput, calls=%fused_computation.17 | convolution fusion | flops 100728832 | bytes 1114112 | tf_op jit(solution)/shard_map/etk,etl->ekl/dot_general | solution.py:31
  105.0 0.2 convert_element_type.41
  105.2 0.0 all-gather.2.cloned.1.call-done
  105.3 2.2 %fusion.148 = f32[8,128]{1,0:T(8,128)} fusion(bf16[8,4096]{1,0:T(8,128)(2,1)S(1)} %convert_element_type.41, bf16[128,4096]{1,0:T(8,128)(2,1)} %all-gather.2.cloned.1.call-done), kind=kOutput, calls=%fused_computation.206 | convolution fusion | flops 8388608 | bytes 1118208 | tf_op jit(solution)/shard_map/dot_general | solution.py:53
  (2 shorter events, 0.0 us)
Async XLA Ops:
  7.4 8.6 %copy-start = (bf16[8,256,512]{2,1,0:T(8,128)(2,1)S(1)}, bf16[8,256,512]{2,1,0:T(8,128)(2,1)}, u32[]{:S(2)}) copy-start(bf16[8,256,512]{2,1,0:T(8,128)(2,1)} %param.8) | copy-start | bytes 6291460
  7.4 95.9 %all-reduce.3.cloned.1.call-start = ((), (), s32[]{:S(2)}) async-start(), calls=%async_computation.1 | async-start | bytes 2097152 | tf_op jit(solution)/shard_map/psum | solution.py:49
  17.6 87.6 %all-gather.2.cloned.1.call-start = ((), (), s32[]{:S(2)}) async-start(), calls=%async_computation | async-start | bytes 1081344 | tf_op jit(solution)/shard_map/all_gather | solution.py:55
Sparse Core Ops, SparseCore 0:
  17.8 85.4 all-reduce.2
Sparse Core Ops, SparseCore 1:
  20.6 54.0 all-gather.1
where the time goes:
time: 115 us
  waiting for transfers between devices  85.6 us (74%)
  between operations  14.9 us (13%)
  matrix products  12 us (10%)
  other arithmetic  2.25 us (2%)
    psum x1, waiting for transfers between devices, on_device(): picked_in, picked_out = lax.psum((term_in, term_out), 'tensor')  85 us
    dot_general x1, matrix products, on_device(): jnp.einsum('etf,fk->etk', activations, in_matrix, preferred_element_type=...  6.33 us
  transfers between devices with their start and end apart: 2, of which 1 were waited for; matrix products, arithmetic and copies ran while one was open for 2% of the time, Pallas kernels for 0%

commit v1 on v0

v1 whole, which is shorter than its diff:
```python
import functools
import math

import jax
import jax.numpy as jnp
from jax import lax
from jax.experimental import pallas as pl
from jax.experimental.pallas import tpu as pltpu
from jax.sharding import PartitionSpec as P

HB = 256
F32, BF16, I32 = jnp.float32, jnp.bfloat16, jnp.int32
VMEM_LIMIT = 40 * 1024 * 1024
VMEM = functools.partial(pl.BlockSpec, memory_space=pltpu.VMEM)
ANY = functools.partial(pl.BlockSpec, memory_space=pl.ANY)


def parity(value):
    for step in (8, 4, 2, 1):
        value = jnp.bitwise_xor(value, jnp.right_shift(value, step))
    return jnp.bitwise_and(value, 1)


def terms_kernel(parts, act_hbm, grad_hbm, sign_in, sign_out, pick_in, pick_out, term_ref, own_ref,
                 act, grad, mat_in, mat_out, sems):
    examples = act.shape[0]
    picks = pick_in.shape[1]
    cols = 2 * picks
    copies = []
    for e in range(examples):
        pair = (
            pltpu.make_async_copy(act_hbm.at[e], act.at[e], sems.at[e, 0]),
            pltpu.make_async_copy(grad_hbm.at[e], grad.at[e], sems.at[e, 1]),
        )
        for copy in pair:
            copy.start()
        copies.append(pair)

    me = lax.axis_index("tensor")
    row = lax.broadcasted_iota(I32, (cols, picks), 0)
    lane = lax.broadcasted_iota(I32, (cols, picks), 1)
    half = picks // 2
    after = row - picks
    from_out = jnp.where(after < half, 2 * after, 2 * (after - half) + 1)
    zero = jnp.zeros((), F32)
    spread = jnp.where(row == lane, pick_in[...].astype(F32), zero) + jnp.where(
        (after >= 0) & (from_out == lane), pick_out[...].astype(F32), zero
    )
    pick = jnp.sum(spread, axis=1, keepdims=True).astype(I32)
    is_in = lax.broadcasted_iota(I32, (cols, 1), 0) < picks

    def part_of(width):
        owner = jnp.zeros_like(pick)
        for q in range(1, parts):
            owner = owner + jnp.where(pick >= q * width, 1, 0)
        return owner, jnp.right_shift(pick - owner * width, 8)

    own_in, block_in = part_of(act.shape[2])
    own_out, block_out = part_of(grad.shape[2])
    owner = jnp.where(is_in, own_in, own_out)
    block_in = jnp.where(is_in, block_in, -1)
    block_out = jnp.where(is_in, -1, block_out)
    offset = lax.broadcasted_iota(I32, (cols, HB), 1)
    odd = jnp.bitwise_xor(
        parity(jnp.bitwise_and(offset, jnp.bitwise_and(pick, HB - 1))),
        parity(jnp.bitwise_and(owner, me)),
    )
    hadamard = (1 - 2 * odd).astype(F32)
    for matrix, signs, blocks in ((mat_in, sign_in, block_in), (mat_out, sign_out, block_out)):
        for j in range(matrix.shape[1] // HB):
            span = slice(j * HB, (j + 1) * HB)
            flips = (2 * signs[:, span] - 1).astype(F32)
            matrix[:, span] = jnp.where(blocks == j, hadamard * flips, zero).astype(BF16)

    contract = (((1,), (1,)), ((), ()))
    for e in range(examples):
        for copy in copies[e]:
            copy.wait()
        total = lax.dot_general(act[e], mat_in[...], contract, preferred_element_type=F32)
        total = total + lax.dot_general(grad[e], mat_out[...], contract, preferred_element_type=F32)
        term_ref[e] = total.astype(BF16)

        @pl.when(me == e)
        def _():
            own_ref[...] = total


def terms(parts, activations, out_grads, signs_in, signs_out, picks_in, picks_out):
    examples, tokens, width_in = activations.shape
    width_out = out_grads.shape[2]
    cols = 2 * picks_in.shape[0]
    return pl.pallas_call(
        functools.partial(terms_kernel, parts),
        out_shape=(
            jax.ShapeDtypeStruct((examples, tokens, cols), BF16),
            jax.ShapeDtypeStruct((tokens, cols), F32),
        ),
        in_specs=[ANY(), ANY()] + [VMEM()] * 4,
        out_specs=(VMEM(), VMEM()),
        scratch_shapes=[
            pltpu.VMEM((examples, tokens, width_in), BF16),
            pltpu.VMEM((examples, tokens, width_out), BF16),
            pltpu.VMEM((cols, width_in), BF16),
            pltpu.VMEM((cols, width_out), BF16),
            pltpu.SemaphoreType.DMA((examples, 2)),
        ],
        compiler_params=pltpu.CompilerParams(vmem_limit_bytes=VMEM_LIMIT),
        cost_estimate=pl.CostEstimate(
            flops=2 * examples * tokens * cols * (width_in + width_out),
            bytes_accessed=2 * examples * tokens * (width_in + width_out),
            transcendentals=0,
        ),
        name="terms",
    )(
        activations,
        out_grads,
        signs_in.reshape(1, -1),
        signs_out.reshape(1, -1),
        picks_in.reshape(1, -1),
        picks_out.reshape(1, -1),
    )


def sketch_kernel(scale, parts_ref, own_ref, out_ref):
    me = lax.axis_index("tensor")
    total = own_ref[...]
    for q in range(parts_ref.shape[0]):
        total = total + jnp.where(me == q, 0.0, parts_ref[q].astype(F32))
    picks = total.shape[1] // 2
    outer = lax.dot_general(
        total, total, (((0,), (0,)), ((), ())), precision=lax.Precision.HIGHEST, preferred_element_type=F32
    )
    half = picks // 2
    sketch = scale * jnp.concatenate(
        [outer[picks : picks + half, :picks], outer[picks + half :, :picks]], axis=1
    )
    for q in range(out_ref.shape[0]):
        out_ref[q] = sketch


def sketch(scale, parts, own):
    count, tokens, cols = parts.shape
    return pl.pallas_call(
        functools.partial(sketch_kernel, scale),
        out_shape=jax.ShapeDtypeStruct((count, cols // 4, cols), F32),
        in_specs=[VMEM(), VMEM()],
        out_specs=VMEM(),
        cost_estimate=pl.CostEstimate(
            flops=12 * tokens * cols * cols, bytes_accessed=2 * count * tokens * cols, transcendentals=0
        ),
        name="sketch",
    )(parts, own)


def scores_kernel(sizes, sketch_ref, *refs):
    tests, out_ref = refs[:-1], refs[-1]
    n_z, n_x, n_c = sizes
    me = lax.axis_index("dp")
    my_z, my_x, my_c = me // (n_x * n_c), (me // n_c) % n_x, me % n_c
    examples = sketch_ref.shape[0]
    total = jnp.zeros((2 * examples, out_ref.shape[1]), F32)
    for c in range(n_c):
        for x in range(n_x):
            for z in range(n_z):
                index = ((my_z + n_z - z) % n_z * n_x + (my_x + n_x - x) % n_x) * n_c + (my_c + c) % n_c
                left = sketch_ref[:, pl.ds(index, 1), :].reshape(examples, -1)
                high = left.astype(BF16).astype(F32)
                both = jnp.concatenate([high, left - high], axis=0).astype(BF16)
                total = total + lax.dot_general(
                    both, tests[c * n_x + x][z], (((1,), (1,)), ((), ())), preferred_element_type=F32
                )
    out_ref[...] = total[:examples] + total[examples:]


def scores(sizes, sketches, tests):
    examples = sketches.shape[0]
    rows = tests[0].shape[1]
    return pl.pallas_call(
        functools.partial(scores_kernel, sizes),
        out_shape=jax.ShapeDtypeStruct((examples, rows), F32),
        in_specs=[VMEM()] * (1 + len(tests)),
        out_specs=VMEM(),
        name="scores",
    )(sketches, *tests)


def shift(value, stride, count, step, size):
    pairs = []
    for i in range(size):
        at = i // stride % count
        pairs.append((i, i + ((at + step) % count - at) * stride))
    return lax.ppermute(value, "dp", pairs)


def gather_tests(block, sizes):
    n_z, n_x, n_c = sizes
    size = n_z * n_x * n_c
    column = jnp.stack([block] + [shift(block, n_x * n_c, n_z, k, size) for k in range(1, n_z)])
    plane = [column] + [shift(column, n_c, n_x, k, size) for k in range(1, n_x)]
    return plane + [shift(column, 1, n_c, 1, size) for column in plane]


def on_device(activations, out_grads, signs_in, signs_out, picks_in, picks_out, test_sketches):
    parts = lax.axis_size("tensor")
    tokens = activations.shape[1]
    sizes = (lax.axis_size("dp") // 8, 4, 2)
    term, own = terms(parts, activations, out_grads, signs_in, signs_out, picks_in, picks_out)
    tests = gather_tests(test_sketches, sizes)
    mine = lax.all_to_all(term, "tensor", 0, 0, tiled=True)
    scale = 1.0 / (HB * parts) / math.sqrt(tokens)
    spread = sketch(scale, mine, own)
    sketches = lax.all_to_all(spread, "tensor", 0, 0, tiled=True)
    return scores(sizes, sketches, tests)


def solution(mesh):
    in_specs = (
        P("dp", None, "tensor"),
        P("dp", None, "tensor"),
        P("tensor"),
        P("tensor"),
        P(),
        P(),
        P("tensor", "dp"),
    )
    out_specs = P("dp", "tensor")
    return jax.shard_map(
        on_device, mesh=mesh, in_specs=in_specs, out_specs=out_specs, check_vma=False
    )
```

time: 115 us -> 61.7 us (0.54)
  waiting for transfers between devices: 85.6 us -> 10.6 us
  starting transfers between devices: 0.05 us -> 27 us
  between operations: 14.9 us -> 0.13 us
  Pallas kernels: 0 us -> 14 us
  matrix products: 12 us -> 0 us
  local copies, waits for them, and re-layouts: 0.18 us -> 9.49 us
  other arithmetic: 2.25 us -> 0.02 us
    psum x1 -> x0, waiting for transfers between devices: 85 us -> none  [on_device(): picked_in, picked_out = lax.psum((term_in, term_out), 'tensor')]
    ppermute x0 -> x10, starting transfers between devices: none -> 15.1 us  [shift(): return lax.ppermute(value, 'dp', pairs)]
    pallas_call x0 -> x3, Pallas kernels: none -> 14 us  [the longest x1 9.22 us: terms(): pl.pallas_call(functools.partial(terms_kernel, parts), out_shape=(jax.Sha...]
    dot_general x4 -> x0, matrix products: 12 us -> none  [the longest x1 6.33 us: on_device(): jnp.einsum('etf,fk->etk', activations, in_matrix, preferred_element_type=...]
    all_to_all x0 -> x2, starting transfers between devices: none -> 11.9 us  [the longest x1 6.08 us: on_device(): sketches = lax.all_to_all(spread, 'tensor', 0, 0, tiled=True)]
    unnamed x2 -> x34, local copies, waits for them, and re-layouts: 0.01 us -> 8.79 us
    ppermute x0 -> x10, waiting for transfers between devices: none -> 6.04 us  [shift(): return lax.ppermute(value, 'dp', pairs)]
    all_to_all x0 -> x2, waiting for transfers between devices: none -> 4.52 us  [the longest x1 4.52 us: on_device(): sketches = lax.all_to_all(spread, 'tensor', 0, 0, tiled=True)]
  transfers between devices with their start and end apart: 2 -> 12, of which waited for: 1 -> 7; matrix products, arithmetic and copies ran while one was open for 2% -> 0% of each run, Pallas kernels for 0% -> 4%
where the time goes in v1:
time: 61.7 us; the launch traced here: 61.2 us
  starting transfers between devices  27 us (44%)
  Pallas kernels  14 us (23%)
  waiting for transfers between devices  10.6 us (17%)
  local copies, waits for them, and re-layouts  9.49 us (15%)
    ppermute x10, starting transfers between devices, shift(): return lax.ppermute(value, 'dp', pairs)  15.1 us
    pallas_call x1, Pallas kernels, terms(): pl.pallas_call(functools.partial(terms_kernel, parts), out_shape=(jax.Sha...  9.22 us
    unnamed x34, local copies, waits for them, and re-layouts  8.79 us
    all_to_all x1, starting transfers between devices, on_device(): sketches = lax.all_to_all(spread, 'tensor', 0, 0, tiled=True)  6.08 us
    ppermute x10, waiting for transfers between devices, shift(): return lax.ppermute(value, 'dp', pairs)  6.04 us
    all_to_all x1, starting transfers between devices, on_device(): mine = lax.all_to_all(term, 'tensor', 0, 0, tiled=True)  5.82 us
    all_to_all x1, waiting for transfers between devices, on_device(): sketches = lax.all_to_all(spread, 'tensor', 0, 0, tiled=True)  4.52 us
    pallas_call x1, Pallas kernels, scores(): pl.pallas_call(functools.partial(scores_kernel, sizes), out_shape=jax.Sha...  2.59 us
  transfers between devices with their start and end apart: 12, of which 7 were waited for; matrix products, arithmetic and copies ran while one was open for 0% of the time, Pallas kernels for 4%

profile of v1, /device:TPU:2, one launch (start us, length us, event | category | flops | bytes accessed | tf_op | source)
XLA Modules:
  0.0 61.2 jit_solution(16600800136876428412)
XLA Ops:
  0.0 0.7 %reshape.12.sign_in = s32[1,1792]{1,0:T(1,128)S(1)} reshape(s32[1792]{0:T(1024)} %param.9) | data formatting | bytes 14336 | tf_op jit(solution)/shard_map/reshape | solution.py:117
  0.7 3.1 %copy-done = bf16[8,256,1792]{2,1,0:T(8,128)(2,1)S(1)} copy-done((bf16[8,256,1792]{2,1,0:T(8,128)(2,1)S(1)}, bf16[8,256,1792]{2,1,0:T(8,128)(2,1)}, u32[]{:S(2)}) %copy-start) | copy-done | bytes 7340056
  3.8 1.6 %copy-done.1 = bf16[8,256,512]{2,1,0:T(8,128)(2,1)S(1)} copy-done((bf16[8,256,512]{2,1,0:T(8,128)(2,1)S(1)}, bf16[8,256,512]{2,1,0:T(8,128)(2,1)}, u32[]{:S(2)}) %copy-start.1) | copy-done | bytes 2097176
  5.4 0.7 %copy-done.3 = s32[512]{0:T(512)S(1)} copy-done((s32[512]{0:T(512)S(1)}, s32[512]{0:T(512)}, u32[]{:S(2)}) %copy-start.3) | copy-done | bytes 2072
  6.1 0.7 %copy-done.4 = s32[64]{0:T(128)S(1)} copy-done((s32[64]{0:T(128)S(1)}, s32[64]{0:T(128)}, u32[]{:S(2)}) %copy-start.4) | copy-done | bytes 280
  6.7 0.7 %copy-done.5 = s32[64]{0:T(128)S(1)} copy-done((s32[64]{0:T(128)S(1)}, s32[64]{0:T(128)}, u32[]{:S(2)}) %copy-start.5) | copy-done | bytes 280
  7.4 9.2 %terms.1 = (bf16[8,256,128]{2,1,0:T(8,128)(2,1)}, f32[256,128]{1,0:T(8,128)S(1)}) custom-call(bf16[8,256,1792]{2,1,0:T(8,128)(2,1)S(1)} %copy-done, bf16[8,256,512]{2,1,0:T(8,128)(2,1)S(1)} %copy-done.1, s32[1,1792]{1,0:T(1,128)S(1)} %reshape.12.sign_in, s32[1,512]{1,0:T(1,128)S(1)} %bitcast.7, s32[1,64]{1,0:T(1,128)S(1)} %bitcast.8, s32[1,64]{1,0:T(1,128)S(1)} %bitcast.9), custom_call_target="tpu_custom_call" | custom-call | flops 1207959552 | bytes 9437184 | tf_op jit(solution)/shard_map/terms/pallas_call | solution.py:92
  16.6 0.6 %copy-done.2 = f32[256,128]{1,0:T(8,128)} copy-done((f32[256,128]{1,0:T(8,128)}, f32[256,128]{1,0:T(8,128)S(1)}, u32[]{:S(2)}) %copy-start.2) | copy-done | bytes 131096
  17.2 5.8 %all-to-all-start = ((bf16[8,256,128]{2,1,0:T(8,128)(2,1)}), bf16[8,256,128]{2,1,0:T(8,128)(2,1)S(1)}, u32[]{:S(2)}, u32[]{:S(2)}) async-start(bf16[8,256,128]{2,1,0:T(8,128)(2,1)} %get-tuple-element.7), calls=%async_computation | async-start | bytes 1048576 | tf_op jit(solution)/shard_map/all_to_all | solution.py:209
  23.1 5.5 %collective-permute-start.2 = (bf16[128,128]{1,0:T(8,128)(2,1)S(1)}, bf16[128,128]{1,0:T(8,128)(2,1)S(1)}, u32[]{:S(2)}, u32[]{:S(2)}) collective-permute-start(bf16[128,128]{1,0:T(8,128)(2,1)S(1)} %copy-done.16), channel_id=1, source_target_pairs={{0,192},{8,200},{16,208},{24,216},{32,224},{40,232},{48,240},{56,2... | collective-permute-start | bytes 98312 | tf_op jit(solution)/shard_map/ppermute | solution.py:192
  28.6 1.4 %collective-permute-start.1 = (bf16[128,128]{1,0:T(8,128)(2,1)S(1)}, bf16[128,128]{1,0:T(8,128)(2,1)S(1)}, u32[]{:S(2)}, u32[]{:S(2)}) collective-permute-start(bf16[128,128]{1,0:T(8,128)(2,1)S(1)} %copy-done.16), channel_id=1, source_target_pairs={{0,128},{8,136},{16,144},{24,152},{32,160},{40,168},{48,176},{56,1... | collective-permute-start | bytes 98312 | tf_op jit(solution)/shard_map/ppermute | solution.py:192
  30.0 2.4 %collective-permute-start = (bf16[128,128]{1,0:T(8,128)(2,1)S(1)}, bf16[128,128]{1,0:T(8,128)(2,1)S(1)}, u32[]{:S(2)}, u32[]{:S(2)}) collective-permute-start(bf16[128,128]{1,0:T(8,128)(2,1)S(1)} %copy-done.16), channel_id=1, source_target_pairs={{0,64},{8,72},{16,80},{24,88},{32,96},{40,104},{48,112},{56,120},{... | collective-permute-start | bytes 98312 | tf_op jit(solution)/shard_map/ppermute | solution.py:192
  32.4 0.0 collective-permute-done.2
  32.4 4.8 %collective-permute-done.1 = bf16[128,128]{1,0:T(8,128)(2,1)S(1)} collective-permute-done((bf16[128,128]{1,0:T(8,128)(2,1)S(1)}, bf16[128,128]{1,0:T(8,128)(2,1)S(1)}, u32[]{:S(2)}, u32[]{:S(2)}) %collective-permute-start.1) | collective-permute-done | bytes 32800 | tf_op jit(solution)/shard_map/ppermute | solution.py:192
  37.2 0.2 collective-permute-done
  37.4 1.6 %collective-permute-start.3 = (bf16[4,128,128]{2,1,0:T(8,128)(2,1)S(1)}, bf16[4,128,128]{2,1,0:T(8,128)(2,1)S(1)}, u32[]{:S(2)}, u32[]{:S(2)}) collective-permute-start(bf16[4,128,128]{2,1,0:T(8,128)(2,1)S(1)} %pad_maximum_fusion.refs_0_), channel_id=1, source_target_pairs={{0,16},{8,24},{16,32},{24,40},{32,48},{40,56},{48,0},{56,8},{64,80... | collective-permute-start | bytes 393224 | tf_op jit(solution)/shard_map/ppermute | solution.py:192
  39.0 1.1 %collective-permute-start.4 = (bf16[4,128,128]{2,1,0:T(8,128)(2,1)S(1)}, bf16[4,128,128]{2,1,0:T(8,128)(2,1)S(1)}, u32[]{:S(2)}, u32[]{:S(2)}) collective-permute-start(bf16[4,128,128]{2,1,0:T(8,128)(2,1)S(1)} %pad_maximum_fusion.refs_0_), channel_id=1, source_target_pairs={{0,32},{8,40},{16,48},{24,56},{32,0},{40,8},{48,16},{56,24},{64,96... | collective-permute-start | bytes 393224 | tf_op jit(solution)/shard_map/ppermute | solution.py:192
  40.1 2.2 %collective-permute-start.5 = (bf16[4,128,128]{2,1,0:T(8,128)(2,1)S(1)}, bf16[4,128,128]{2,1,0:T(8,128)(2,1)S(1)}, u32[]{:S(2)}, u32[]{:S(2)}) collective-permute-start(bf16[4,128,128]{2,1,0:T(8,128)(2,1)S(1)} %pad_maximum_fusion.refs_0_), channel_id=1, source_target_pairs={{0,48},{8,56},{16,0},{24,8},{32,16},{40,24},{48,32},{56,40},{64,11... | collective-permute-start | bytes 393224 | tf_op jit(solution)/shard_map/ppermute | solution.py:192
  42.3 0.0 all-to-all-done.parts_ref
  42.3 0.8 %copy-done.6 = bf16[8,256,128]{2,1,0:T(8,128)(2,1)} copy-done((bf16[8,256,128]{2,1,0:T(8,128)(2,1)}, bf16[8,256,128]{2,1,0:T(8,128)(2,1)S(1)}, u32[]{:S(2)}) %copy-start.6) | copy-done | bytes 524312
  43.1 2.2 %sketch.1 = f32[8,32,128]{2,1,0:T(8,128)} custom-call(bf16[8,256,128]{2,1,0:T(8,128)(2,1)} %copy-done.6, f32[256,128]{1,0:T(8,128)} %copy-done.2), custom_call_target="tpu_custom_call" | custom-call | flops 50331648 | bytes 524288 | tf_op jit(solution)/shard_map/sketch/pallas_call | solution.py:143
  45.3 6.1 %all-to-all-start.1 = ((f32[8,32,128]{2,1,0:T(8,128)}), f32[8,32,128]{2,1,0:T(8,128)S(1)}, u32[]{:S(2)}, u32[]{:S(2)}) async-start(f32[8,32,128]{2,1,0:T(8,128)} %sketch.1), calls=%async_computation.1 | async-start | bytes 262144 | tf_op jit(solution)/shard_map/all_to_all | solution.py:212
  51.4 0.5 collective-permute-start.7
  51.9 0.1 collective-permute-start.8
  52.0 0.4 collective-permute-start.9
  52.4 0.3 collective-permute-done.6.refs_4_
  52.7 0.2 collective-permute-done.7.refs_5_
  52.9 0.3 collective-permute-done.8.refs_6_
  53.2 0.2 collective-permute-done.9.refs_7_
  53.4 4.5 %all-to-all-done.1.sketch_ref = f32[8,32,128]{2,1,0:T(8,128)S(1)} async-done(((f32[8,32,128]{2,1,0:T(8,128)}), f32[8,32,128]{2,1,0:T(8,128)S(1)}, u32[]{:S(2)}, u32[]{:S(2)}) %all-to-all-start.1) | async-done | bytes 131104 | tf_op jit(solution)/shard_map/all_to_all | solution.py:212
  58.0 0.6 %copy-done.8 = f32[8,32,128]{2,1,0:T(8,128)} copy-done((f32[8,32,128]{2,1,0:T(8,128)}, f32[8,32,128]{2,1,0:T(8,128)S(1)}, u32[]{:S(2)}) %copy-start.8) | copy-done | bytes 131096
  58.6 2.6 %scores.1 = f32[8,128]{1,0:T(8,128)} custom-call(f32[8,32,128]{2,1,0:T(8,128)} %copy-done.8, bf16[4,128,128]{2,1,0:T(8,128)(2,1)} %copy-done.7, bf16[4,128,128]{2,1,0:T(8,128)(2,1)} %copy-done.9, bf16[4,128,128]{2,1,0:T(8,128)(2,1)} %copy-done.10, bf16[4,128,128]{2,1,0:T(8,128)(2,1)} %copy-done.11, bf16[4,128,128]{2,1,0:T(8,128)(2,1)} %copy-done.12, ...), custom_call_target="tpu_custom_call" | custom-call | tf_op jit(solution)/shard_map/scores/pallas_call | solution.py:178
  (31 shorter events, 0.1 us)
Async XLA Ops:
  0.7 3.1 %copy-start = (bf16[8,256,1792]{2,1,0:T(8,128)(2,1)S(1)}, bf16[8,256,1792]{2,1,0:T(8,128)(2,1)}, u32[]{:S(2)}) copy-start(bf16[8,256,1792]{2,1,0:T(8,128)(2,1)} %act_hbm.1) | copy-start | bytes 22020100
  3.8 1.6 %copy-start.1 = (bf16[8,256,512]{2,1,0:T(8,128)(2,1)S(1)}, bf16[8,256,512]{2,1,0:T(8,128)(2,1)}, u32[]{:S(2)}) copy-start(bf16[8,256,512]{2,1,0:T(8,128)(2,1)} %grad_hbm.1) | copy-start | bytes 6291460
  5.4 0.7 %copy-start.3 = (s32[512]{0:T(512)S(1)}, s32[512]{0:T(512)}, u32[]{:S(2)}) copy-start(s32[512]{0:T(512)} %param.10) | copy-start | bytes 6148
  6.1 0.7 %copy-start.4 = (s32[64]{0:T(128)S(1)}, s32[64]{0:T(128)}, u32[]{:S(2)}) copy-start(s32[64]{0:T(128)} %param.11) | copy-start | bytes 772
  6.7 0.7 %copy-start.5 = (s32[64]{0:T(128)S(1)}, s32[64]{0:T(128)}, u32[]{:S(2)}) copy-start(s32[64]{0:T(128)} %param.12) | copy-start | bytes 772
  7.4 15.7 %copy-start.16 = (bf16[128,128]{1,0:T(8,128)(2,1)S(1)}, bf16[128,128]{1,0:T(8,128)(2,1)}, u32[]{:S(2)}) copy-start(bf16[128,128]{1,0:T(8,128)(2,1)} %param.13) | copy-start | bytes 98308
  16.6 0.6 %copy-start.2 = (f32[256,128]{1,0:T(8,128)}, f32[256,128]{1,0:T(8,128)S(1)}, u32[]{:S(2)}) copy-start(f32[256,128]{1,0:T(8,128)S(1)} %get-tuple-element.8.own_ref) | copy-start | bytes 393220
  17.2 25.0 %all-to-all-start = ((bf16[8,256,128]{2,1,0:T(8,128)(2,1)}), bf16[8,256,128]{2,1,0:T(8,128)(2,1)S(1)}, u32[]{:S(2)}, u32[]{:S(2)}) async-start(bf16[8,256,128]{2,1,0:T(8,128)(2,1)} %get-tuple-element.7), calls=%async_computation | async-start | bytes 1048576 | tf_op jit(solution)/shard_map/all_to_all | solution.py:209
  23.1 9.3 %collective-permute-start.2 = (bf16[128,128]{1,0:T(8,128)(2,1)S(1)}, bf16[128,128]{1,0:T(8,128)(2,1)S(1)}, u32[]{:S(2)}, u32[]{:S(2)}) collective-permute-start(bf16[128,128]{1,0:T(8,128)(2,1)S(1)} %copy-done.16), channel_id=1, source_target_pairs={{0,192},{8,200},{16,208},{24,216},{32,224},{40,232},{48,240},{56,2... | collective-permute-start | bytes 98312 | tf_op jit(solution)/shard_map/ppermute | solution.py:192
  28.6 8.6 %collective-permute-start.1 = (bf16[128,128]{1,0:T(8,128)(2,1)S(1)}, bf16[128,128]{1,0:T(8,128)(2,1)S(1)}, u32[]{:S(2)}, u32[]{:S(2)}) collective-permute-start(bf16[128,128]{1,0:T(8,128)(2,1)S(1)} %copy-done.16), channel_id=1, source_target_pairs={{0,128},{8,136},{16,144},{24,152},{32,160},{40,168},{48,176},{56,1... | collective-permute-start | bytes 98312 | tf_op jit(solution)/shard_map/ppermute | solution.py:192
  30.0 7.4 %collective-permute-start = (bf16[128,128]{1,0:T(8,128)(2,1)S(1)}, bf16[128,128]{1,0:T(8,128)(2,1)S(1)}, u32[]{:S(2)}, u32[]{:S(2)}) collective-permute-start(bf16[128,128]{1,0:T(8,128)(2,1)S(1)} %copy-done.16), channel_id=1, source_target_pairs={{0,64},{8,72},{16,80},{24,88},{32,96},{40,104},{48,112},{56,120},{... | collective-permute-start | bytes 98312 | tf_op jit(solution)/shard_map/ppermute | solution.py:192
  37.4 20.5 %copy-start.7 = (bf16[4,128,128]{2,1,0:T(8,128)(2,1)}, bf16[4,128,128]{2,1,0:T(8,128)(2,1)S(1)}, u32[]{:S(2)}) copy-start(bf16[4,128,128]{2,1,0:T(8,128)(2,1)S(1)} %pad_maximum_fusion.refs_0_) | copy-start | bytes 393220
  37.4 13.9 %collective-permute-start.3 = (bf16[4,128,128]{2,1,0:T(8,128)(2,1)S(1)}, bf16[4,128,128]{2,1,0:T(8,128)(2,1)S(1)}, u32[]{:S(2)}, u32[]{:S(2)}) collective-permute-start(bf16[4,128,128]{2,1,0:T(8,128)(2,1)S(1)} %pad_maximum_fusion.refs_0_), channel_id=1, source_target_pairs={{0,16},{8,24},{16,32},{24,40},{32,48},{40,56},{48,0},{56,8},{64,80... | collective-permute-start | bytes 393224 | tf_op jit(solution)/shard_map/ppermute | solution.py:192
  39.0 12.9 %collective-permute-start.4 = (bf16[4,128,128]{2,1,0:T(8,128)(2,1)S(1)}, bf16[4,128,128]{2,1,0:T(8,128)(2,1)S(1)}, u32[]{:S(2)}, u32[]{:S(2)}) collective-permute-start(bf16[4,128,128]{2,1,0:T(8,128)(2,1)S(1)} %pad_maximum_fusion.refs_0_), channel_id=1, source_target_pairs={{0,32},{8,40},{16,48},{24,56},{32,0},{40,8},{48,16},{56,24},{64,96... | collective-permute-start | bytes 393224 | tf_op jit(solution)/shard_map/ppermute | solution.py:192
  40.1 11.9 %collective-permute-start.5 = (bf16[4,128,128]{2,1,0:T(8,128)(2,1)S(1)}, bf16[4,128,128]{2,1,0:T(8,128)(2,1)S(1)}, u32[]{:S(2)}, u32[]{:S(2)}) collective-permute-start(bf16[4,128,128]{2,1,0:T(8,128)(2,1)S(1)} %pad_maximum_fusion.refs_0_), channel_id=1, source_target_pairs={{0,48},{8,56},{16,0},{24,8},{32,16},{40,24},{48,32},{56,40},{64,11... | collective-permute-start | bytes 393224 | tf_op jit(solution)/shard_map/ppermute | solution.py:192
  42.3 0.8 %copy-start.6 = (bf16[8,256,128]{2,1,0:T(8,128)(2,1)}, bf16[8,256,128]{2,1,0:T(8,128)(2,1)S(1)}, u32[]{:S(2)}) copy-start(bf16[8,256,128]{2,1,0:T(8,128)(2,1)S(1)} %all-to-all-done.parts_ref) | copy-start | bytes 1572868
  45.3 12.7 %all-to-all-start.1 = ((f32[8,32,128]{2,1,0:T(8,128)}), f32[8,32,128]{2,1,0:T(8,128)S(1)}, u32[]{:S(2)}, u32[]{:S(2)}) async-start(f32[8,32,128]{2,1,0:T(8,128)} %sketch.1), calls=%async_computation.1 | async-start | bytes 262144 | tf_op jit(solution)/shard_map/all_to_all | solution.py:212
  51.3 1.3 %collective-permute-start.6 = (bf16[4,128,128]{2,1,0:T(8,128)(2,1)S(1)}, bf16[4,128,128]{2,1,0:T(8,128)(2,1)S(1)}, u32[]{:S(2)}, u32[]{:S(2)}) collective-permute-start(bf16[4,128,128]{2,1,0:T(8,128)(2,1)S(1)} %pad_maximum_fusion.refs_0_), channel_id=1, source_target_pairs={{0,8},{8,0},{16,24},{24,16},{32,40},{40,32},{48,56},{56,48},{64,72... | collective-permute-start | bytes 393224 | tf_op jit(solution)/shard_map/ppermute | solution.py:192
  51.4 6.6 %copy-start.9 = (bf16[4,128,128]{2,1,0:T(8,128)(2,1)}, bf16[4,128,128]{2,1,0:T(8,128)(2,1)S(1)}, u32[]{:S(2)}) copy-start(bf16[4,128,128]{2,1,0:T(8,128)(2,1)S(1)} %collective-permute-done.3.refs_1_) | copy-start | bytes 393220
  51.4 1.5 %collective-permute-start.7 = (bf16[4,128,128]{2,1,0:T(8,128)(2,1)S(1)}, bf16[4,128,128]{2,1,0:T(8,128)(2,1)S(1)}, u32[]{:S(2)}, u32[]{:S(2)}) collective-permute-start(bf16[4,128,128]{2,1,0:T(8,128)(2,1)S(1)} %collective-permute-done.3.refs_1_), channel_id=1, source_target_pairs={{0,8},{8,0},{16,24},{24,16},{32,40},{40,32},{48,56},{56,48},{64,72... | collective-permute-start | bytes 393224 | tf_op jit(solution)/shard_map/ppermute | solution.py:192
  51.9 6.1 %copy-start.10 = (bf16[4,128,128]{2,1,0:T(8,128)(2,1)}, bf16[4,128,128]{2,1,0:T(8,128)(2,1)S(1)}, u32[]{:S(2)}) copy-start(bf16[4,128,128]{2,1,0:T(8,128)(2,1)S(1)} %collective-permute-done.4.refs_2_) | copy-start | bytes 393220
  51.9 1.3 %collective-permute-start.8 = (bf16[4,128,128]{2,1,0:T(8,128)(2,1)S(1)}, bf16[4,128,128]{2,1,0:T(8,128)(2,1)S(1)}, u32[]{:S(2)}, u32[]{:S(2)}) collective-permute-start(bf16[4,128,128]{2,1,0:T(8,128)(2,1)S(1)} %collective-permute-done.4.refs_2_), channel_id=1, source_target_pairs={{0,8},{8,0},{16,24},{24,16},{32,40},{40,32},{48,56},{56,48},{64,72... | collective-permute-start | bytes 393224 | tf_op jit(solution)/shard_map/ppermute | solution.py:192
  52.0 6.0 %copy-start.11 = (bf16[4,128,128]{2,1,0:T(8,128)(2,1)}, bf16[4,128,128]{2,1,0:T(8,128)(2,1)S(1)}, u32[]{:S(2)}) copy-start(bf16[4,128,128]{2,1,0:T(8,128)(2,1)S(1)} %collective-permute-done.5.refs_3_) | copy-start | bytes 393220
  52.0 1.4 %collective-permute-start.9 = (bf16[4,128,128]{2,1,0:T(8,128)(2,1)S(1)}, bf16[4,128,128]{2,1,0:T(8,128)(2,1)S(1)}, u32[]{:S(2)}, u32[]{:S(2)}) collective-permute-start(bf16[4,128,128]{2,1,0:T(8,128)(2,1)S(1)} %collective-permute-done.5.refs_3_), channel_id=1, source_target_pairs={{0,8},{8,0},{16,24},{24,16},{32,40},{40,32},{48,56},{56,48},{64,72... | collective-permute-start | bytes 393224 | tf_op jit(solution)/shard_map/ppermute | solution.py:192
  52.7 5.3 %copy-start.12 = (bf16[4,128,128]{2,1,0:T(8,128)(2,1)}, bf16[4,128,128]{2,1,0:T(8,128)(2,1)S(1)}, u32[]{:S(2)}) copy-start(bf16[4,128,128]{2,1,0:T(8,128)(2,1)S(1)} %collective-permute-done.6.refs_4_) | copy-start | bytes 393220
  52.9 5.1 %copy-start.13 = (bf16[4,128,128]{2,1,0:T(8,128)(2,1)}, bf16[4,128,128]{2,1,0:T(8,128)(2,1)S(1)}, u32[]{:S(2)}) copy-start(bf16[4,128,128]{2,1,0:T(8,128)(2,1)S(1)} %collective-permute-done.7.refs_5_) | copy-start | bytes 393220
  53.2 4.8 %copy-start.14 = (bf16[4,128,128]{2,1,0:T(8,128)(2,1)}, bf16[4,128,128]{2,1,0:T(8,128)(2,1)S(1)}, u32[]{:S(2)}) copy-start(bf16[4,128,128]{2,1,0:T(8,128)(2,1)S(1)} %collective-permute-done.8.refs_6_) | copy-start | bytes 393220
  53.4 4.6 %copy-start.15 = (bf16[4,128,128]{2,1,0:T(8,128)(2,1)}, bf16[4,128,128]{2,1,0:T(8,128)(2,1)S(1)}, u32[]{:S(2)}) copy-start(bf16[4,128,128]{2,1,0:T(8,128)(2,1)S(1)} %collective-permute-done.9.refs_7_) | copy-start | bytes 393220
  58.0 0.7 %copy-start.8 = (f32[8,32,128]{2,1,0:T(8,128)}, f32[8,32,128]{2,1,0:T(8,128)S(1)}, u32[]{:S(2)}) copy-start(f32[8,32,128]{2,1,0:T(8,128)S(1)} %all-to-all-done.1.sketch_ref) | copy-start | bytes 393220

commit v2 on v1

--- a/solution.py
+++ b/solution.py
@@ -10,9 +10,10 @@
 
 HB = 256
 F32, BF16, I32 = jnp.float32, jnp.bfloat16, jnp.int32
-VMEM_LIMIT = 40 * 1024 * 1024
+MIB = 1024 * 1024
+AHEAD = 3
 VMEM = functools.partial(pl.BlockSpec, memory_space=pltpu.VMEM)
-ANY = functools.partial(pl.BlockSpec, memory_space=pl.ANY)
+HBM = functools.partial(pl.BlockSpec, memory_space=pltpu.HBM)
 
 
 def parity(value):
@@ -21,21 +22,37 @@
     return jnp.bitwise_and(value, 1)
 
 
-def terms_kernel(parts, act_hbm, grad_hbm, sign_in, sign_out, pick_in, pick_out, term_ref, own_ref,
-                 act, grad, mat_in, mat_out, sems):
+def terms_kernel(parts, act_hbm, grad_hbm, sign_in_hbm, sign_out_hbm, pick_in_hbm, pick_out_hbm, term_hbm, own_hbm,
+                 act, grad, term, own, sign_in, sign_out, pick_in, pick_out, mat_in, mat_out, sems, send_sems, small_sems):
     examples = act.shape[0]
-    picks = pick_in.shape[1]
+    picks = pick_in.shape[0]
     cols = 2 * picks
+    small = [
+        pltpu.make_async_copy(source, target, small_sems.at[i])
+        for i, (source, target) in enumerate(
+            (
+                (pick_in_hbm, pick_in),
+                (pick_out_hbm, pick_out),
+                (sign_in_hbm, sign_in),
+                (sign_out_hbm, sign_out),
+            )
+        )
+    ]
+    for copy in small:
+        copy.start()
     copies = []
     for e in range(examples):
         pair = (
             pltpu.make_async_copy(act_hbm.at[e], act.at[e], sems.at[e, 0]),
             pltpu.make_async_copy(grad_hbm.at[e], grad.at[e], sems.at[e, 1]),
         )
-        for copy in pair:
-            copy.start()
+        if e < AHEAD:
+            for copy in pair:
+                copy.start()
         copies.append(pair)
 
+    for copy in small:
+        copy.wait()
     me = lax.axis_index("tensor")
     row = lax.broadcasted_iota(I32, (cols, picks), 0)
     lane = lax.broadcasted_iota(I32, (cols, picks), 1)
@@ -43,8 +60,8 @@
     after = row - picks
     from_out = jnp.where(after < half, 2 * after, 2 * (after - half) + 1)
     zero = jnp.zeros((), F32)
-    spread = jnp.where(row == lane, pick_in[...].astype(F32), zero) + jnp.where(
-        (after >= 0) & (from_out == lane), pick_out[...].astype(F32), zero
+    spread = jnp.where(row == lane, pick_in[...].reshape(1, picks).astype(F32), zero) + jnp.where(
+        (after >= 0) & (from_out == lane), pick_out[...].reshape(1, picks).astype(F32), zero
     )
     pick = jnp.sum(spread, axis=1, keepdims=True).astype(I32)
     is_in = lax.broadcasted_iota(I32, (cols, 1), 0) < picks
@@ -67,22 +84,32 @@
     )
     hadamard = (1 - 2 * odd).astype(F32)
     for matrix, signs, blocks in ((mat_in, sign_in, block_in), (mat_out, sign_out, block_out)):
-        for j in range(matrix.shape[1] // HB):
+        for j in range(matrix.shape[0] // HB):
             span = slice(j * HB, (j + 1) * HB)
-            flips = (2 * signs[:, span] - 1).astype(F32)
-            matrix[:, span] = jnp.where(blocks == j, hadamard * flips, zero).astype(BF16)
-
-    contract = (((1,), (1,)), ((), ()))
+            flips = (2 * signs[span].reshape(1, HB) - 1).astype(F32)
+            matrix[span, :] = jnp.where(blocks == j, hadamard * flips, zero).T.astype(BF16)
+
+    sends = []
     for e in range(examples):
         for copy in copies[e]:
             copy.wait()
-        total = lax.dot_general(act[e], mat_in[...], contract, preferred_element_type=F32)
-        total = total + lax.dot_general(grad[e], mat_out[...], contract, preferred_element_type=F32)
-        term_ref[e] = total.astype(BF16)
+        if e + AHEAD < examples:
+            for copy in copies[e + AHEAD]:
+                copy.start()
+        total = jnp.dot(act[e], mat_in[...], preferred_element_type=F32)
+        total = total + jnp.dot(grad[e], mat_out[...], preferred_element_type=F32)
+        term[e] = total.astype(BF16)
+        sends.append(pltpu.make_async_copy(term.at[e], term_hbm.at[e], send_sems.at[e]))
+        sends[e].start()
 
         @pl.when(me == e)
         def _():
-            own_ref[...] = total
+            own[...] = total
+
+    sends.append(pltpu.make_async_copy(own, own_hbm, send_sems.at[examples]))
+    sends[-1].start()
+    for copy in sends:
+        copy.wait()
 
 
 def terms(parts, activations, out_grads, signs_in, signs_out, picks_in, picks_out):
@@ -95,37 +122,39 @@
             jax.ShapeDtypeStruct((examples, tokens, cols), BF16),
             jax.ShapeDtypeStruct((tokens, cols), F32),
         ),
-        in_specs=[ANY(), ANY()] + [VMEM()] * 4,
-        out_specs=(VMEM(), VMEM()),
+        in_specs=[HBM()] * 6,
+        out_specs=(HBM(), HBM()),
         scratch_shapes=[
             pltpu.VMEM((examples, tokens, width_in), BF16),
             pltpu.VMEM((examples, tokens, width_out), BF16),
-            pltpu.VMEM((cols, width_in), BF16),
-            pltpu.VMEM((cols, width_out), BF16),
+            pltpu.VMEM((examples, tokens, cols), BF16),
+            pltpu.VMEM((tokens, cols), F32),
+            pltpu.VMEM(signs_in.shape, I32),
+            pltpu.VMEM(signs_out.shape, I32),
+            pltpu.VMEM(picks_in.shape, I32),
+            pltpu.VMEM(picks_out.shape, I32),
+            pltpu.VMEM((width_in, cols), BF16),
+            pltpu.VMEM((width_out, cols), BF16),
             pltpu.SemaphoreType.DMA((examples, 2)),
+            pltpu.SemaphoreType.DMA((examples + 1,)),
+            pltpu.SemaphoreType.DMA((4,)),
         ],
-        compiler_params=pltpu.CompilerParams(vmem_limit_bytes=VMEM_LIMIT),
+        compiler_params=pltpu.CompilerParams(vmem_limit_bytes=63 * MIB),
         cost_estimate=pl.CostEstimate(
             flops=2 * examples * tokens * cols * (width_in + width_out),
             bytes_accessed=2 * examples * tokens * (width_in + width_out),
             transcendentals=0,
         ),
         name="terms",
-    )(
-        activations,
-        out_grads,
-        signs_in.reshape(1, -1),
-        signs_out.reshape(1, -1),
-        picks_in.reshape(1, -1),
-        picks_out.reshape(1, -1),
-    )
+    )(activations, out_grads, signs_in, signs_out, picks_in, picks_out)
 
 
 def sketch_kernel(scale, parts_ref, own_ref, out_ref):
     me = lax.axis_index("tensor")
-    total = own_ref[...]
+    total = jnp.zeros(own_ref.shape, F32)
     for q in range(parts_ref.shape[0]):
         total = total + jnp.where(me == q, 0.0, parts_ref[q].astype(F32))
+    total = total + 2.0 * own_ref[...]
     picks = total.shape[1] // 2
     outer = lax.dot_general(
         total, total, (((0,), (0,)), ((), ())), precision=lax.Precision.HIGHEST, preferred_element_type=F32
@@ -148,6 +177,7 @@
         cost_estimate=pl.CostEstimate(
             flops=12 * tokens * cols * cols, bytes_accessed=2 * count * tokens * cols, transcendentals=0
         ),
+        compiler_params=pltpu.CompilerParams(vmem_limit_bytes=8 * MIB),
         name="sketch",
     )(parts, own)
 
@@ -162,7 +192,7 @@
     for c in range(n_c):
         for x in range(n_x):
             for z in range(n_z):
-                index = ((my_z + n_z - z) % n_z * n_x + (my_x + n_x - x) % n_x) * n_c + (my_c + c) % n_c
+                index = (flip(my_z, z) * n_x + flip(my_x, x)) * n_c + (my_c + c) % n_c
                 left = sketch_ref[:, pl.ds(index, 1), :].reshape(examples, -1)
                 high = left.astype(BF16).astype(F32)
                 both = jnp.concatenate([high, left - high], axis=0).astype(BF16)
@@ -180,24 +210,22 @@
         out_shape=jax.ShapeDtypeStruct((examples, rows), F32),
         in_specs=[VMEM()] * (1 + len(tests)),
         out_specs=VMEM(),
+        compiler_params=pltpu.CompilerParams(vmem_limit_bytes=8 * MIB),
         name="scores",
     )(sketches, *tests)
 
 
-def shift(value, stride, count, step, size):
+def flip(at, which):
+    pair = lambda value: value + 1 - 2 * (value % 2)
+    return (at, pair(at), 3 - at, pair(3 - at))[which]
+
+
+def swap(value, stride, count, which, size):
     pairs = []
     for i in range(size):
         at = i // stride % count
-        pairs.append((i, i + ((at + step) % count - at) * stride))
+        pairs.append((i, i + (flip(at, which) - at) * stride))
     return lax.ppermute(value, "dp", pairs)
-
-
-def gather_tests(block, sizes):
-    n_z, n_x, n_c = sizes
-    size = n_z * n_x * n_c
-    column = jnp.stack([block] + [shift(block, n_x * n_c, n_z, k, size) for k in range(1, n_z)])
-    plane = [column] + [shift(column, n_c, n_x, k, size) for k in range(1, n_x)]
-    return plane + [shift(column, 1, n_c, 1, size) for column in plane]
 
 
 def on_device(activations, out_grads, signs_in, signs_out, picks_in, picks_out, test_sketches):
@@ -205,10 +233,16 @@
     tokens = activations.shape[1]
     sizes = (lax.axis_size("dp") // 8, 4, 2)
     term, own = terms(parts, activations, out_grads, signs_in, signs_out, picks_in, picks_out)
-    tests = gather_tests(test_sketches, sizes)
+    n_z, n_x, n_c = sizes
+    devices = n_z * n_x * n_c
+    column = [test_sketches] + [swap(test_sketches, n_x * n_c, n_z, k, devices) for k in (1, 2, 3)]
+    term, *column = lax.optimization_barrier((term, *column))
+    column = jnp.stack(column)
+    plane = [column] + [swap(column, n_c, n_x, k, devices) for k in (1, 2, 3)]
+    tests = plane + [swap(part, 1, n_c, 1, devices) for part in plane]
     mine = lax.all_to_all(term, "tensor", 0, 0, tiled=True)
     scale = 1.0 / (HB * parts) / math.sqrt(tokens)
-    spread = sketch(scale, mine, own)
+    spread = sketch(scale, mine, 0.5 * own)
     sketches = lax.all_to_all(spread, "tensor", 0, 0, tiled=True)
     return scores(sizes, sketches, tests)
 

time: 61.7 us -> 42.4 us (0.69)
  local copies, waits for them, and re-layouts: 9.49 us -> 0.01 us
  Pallas kernels: 14 us -> 9.42 us
  starting transfers between devices: 27 us -> 22.9 us
  waiting for transfers between devices: 10.6 us -> 8.78 us
  other arithmetic: 0.02 us -> 0.93 us
    unnamed x34 -> x2, local copies, waits for them, and re-layouts: 8.79 us -> 0.01 us
    ppermute x10, waiting for transfers between devices: 6.04 us -> 1.04 us  [swap(): return lax.ppermute(value, 'dp', pairs)]
    all_to_all x1, waiting for transfers between devices: 0.01 us -> 3.37 us  [on_device(): mine = lax.all_to_all(term, 'tensor', 0, 0, tiled=True)]
    all_to_all x1, starting transfers between devices: 6.08 us -> 3.37 us  [on_device(): sketches = lax.all_to_all(spread, 'tensor', 0, 0, tiled=True)]
    pallas_call x1, Pallas kernels: 9.22 us -> 7.02 us  [terms(): pl.pallas_call(functools.partial(terms_kernel, parts), out_shape=(jax.Sha...]
    pallas_call x1, Pallas kernels: 2.59 us -> 1.27 us  [scores(): pl.pallas_call(functools.partial(scores_kernel, sizes), out_shape=jax.Sha...]
    pallas_call x1, Pallas kernels: 2.19 us -> 1.13 us  [sketch(): pl.pallas_call(functools.partial(sketch_kernel, scale), out_shape=jax.Sha...]
    mul x0 -> x1, other arithmetic: none -> 0.91 us  [on_device(): spread = sketch(scale, mine, 0.5 * own)]
  transfers between devices with their start and end apart: 12 -> 12, of which waited for: 7 -> 6; matrix products, arithmetic and copies ran while one was open for 0% -> 2% of each run, Pallas kernels for 4% -> 19%
where the time goes in v2:
time: 42.4 us; the launch traced here: 42.1 us
  starting transfers between devices  22.9 us (54%)
  Pallas kernels  9.42 us (22%)
  waiting for transfers between devices  8.78 us (21%)
  other arithmetic  0.93 us (2%)
    ppermute x10, starting transfers between devices, swap(): return lax.ppermute(value, 'dp', pairs)  14.6 us
    pallas_call x1, Pallas kernels, terms(): pl.pallas_call(functools.partial(terms_kernel, parts), out_shape=(jax.Sha...  7.02 us
    all_to_all x1, starting transfers between devices, on_device(): mine = lax.all_to_all(term, 'tensor', 0, 0, tiled=True)  4.93 us
    all_to_all x1, waiting for transfers between devices, on_device(): sketches = lax.all_to_all(spread, 'tensor', 0, 0, tiled=True)  4.38 us
    all_to_all x1, waiting for transfers between devices, on_device(): mine = lax.all_to_all(term, 'tensor', 0, 0, tiled=True)  3.37 us
    all_to_all x1, starting transfers between devices, on_device(): sketches = lax.all_to_all(spread, 'tensor', 0, 0, tiled=True)  3.37 us
    pallas_call x1, Pallas kernels, scores(): pl.pallas_call(functools.partial(scores_kernel, sizes), out_shape=jax.Sha...  1.27 us
    pallas_call x1, Pallas kernels, sketch(): pl.pallas_call(functools.partial(sketch_kernel, scale), out_shape=jax.Sha...  1.13 us
  transfers between devices with their start and end apart: 12, of which 6 were waited for; matrix products, arithmetic and copies ran while one was open for 2% of the time, Pallas kernels for 19%

profile of v2, /device:TPU:2, one launch (start us, length us, event | category | flops | bytes accessed | tf_op | source)
XLA Modules:
  0.0 42.1 jit_solution(13069561416948953472)
XLA Ops:
  0.0 0.0 copy-start
  0.0 6.3 %collective-permute-start.1 = (bf16[128,128]{1,0:T(8,128)(2,1)}, bf16[128,128]{1,0:T(8,128)(2,1)S(1)}, u32[]{:S(2)}, u32[]{:S(2)}) collective-permute-start(bf16[128,128]{1,0:T(8,128)(2,1)} %param.13), channel_id=1, source_target_pairs={{0,192},{8,200},{16,208},{24,216},{32,224},{40,232},{48,240},{56,2... | collective-permute-start | bytes 98312 | tf_op jit(solution)/shard_map/ppermute | solution.py:228
  6.3 1.5 %collective-permute-start = (bf16[128,128]{1,0:T(8,128)(2,1)}, bf16[128,128]{1,0:T(8,128)(2,1)S(1)}, u32[]{:S(2)}, u32[]{:S(2)}) collective-permute-start(bf16[128,128]{1,0:T(8,128)(2,1)} %param.13), channel_id=1, source_target_pairs={{0,64},{8,72},{16,80},{24,88},{32,96},{40,104},{48,112},{56,120},{... | collective-permute-start | bytes 98312 | tf_op jit(solution)/shard_map/ppermute | solution.py:228
  7.8 1.0 %collective-permute-start.2 = (bf16[128,128]{1,0:T(8,128)(2,1)}, bf16[128,128]{1,0:T(8,128)(2,1)S(1)}, u32[]{:S(2)}, u32[]{:S(2)}) collective-permute-start(bf16[128,128]{1,0:T(8,128)(2,1)} %param.13), channel_id=1, source_target_pairs={{0,128},{8,136},{16,144},{24,152},{32,160},{40,168},{48,176},{56,1... | collective-permute-start | bytes 98312 | tf_op jit(solution)/shard_map/ppermute | solution.py:228
  8.8 7.0 %terms.1 = (bf16[8,256,128]{2,1,0:T(8,128)(2,1)}, f32[256,128]{1,0:T(8,128)}) custom-call(bf16[8,256,1792]{2,1,0:T(8,128)(2,1)} %act_hbm.1, bf16[8,256,512]{2,1,0:T(8,128)(2,1)} %grad_hbm.1, s32[1792]{0:T(1024)} %sign_in_hbm.1, s32[512]{0:T(512)} %sign_out_hbm.1, s32[64]{0:T(128)} %pick_in_hbm.1, s32[64]{0:T(128)} %pick_out_hbm.1), custom_call_target="tpu_custom_call" | custom-call | flops 1207959552 | bytes 9437184 | tf_op jit(solution)/shard_map/terms/pallas_call | solution.py:119
  15.8 0.0 collective-permute-done.1
  15.8 0.0 collective-permute-done
  15.8 0.0 collective-permute-done.2
  15.8 4.9 %all-to-all-start = ((bf16[8,256,128]{2,1,0:T(8,128)(2,1)}), bf16[8,256,128]{2,1,0:T(8,128)(2,1)S(1)}, u32[]{:S(2)}, u32[]{:S(2)}) async-start(bf16[8,256,128]{2,1,0:T(8,128)(2,1)} %get-tuple-element.13), calls=%async_computation | async-start | bytes 1048576 | tf_op jit(solution)/shard_map/all_to_all | solution.py:243
  20.7 0.0 copy-done
  20.8 2.2 %collective-permute-start.5 = (bf16[4,128,128]{2,1,0:T(8,128)(2,1)S(1)}, bf16[4,128,128]{2,1,0:T(8,128)(2,1)S(1)}, u32[]{:S(2)}, u32[]{:S(2)}) collective-permute-start(bf16[4,128,128]{2,1,0:T(8,128)(2,1)S(1)} %pad_maximum_fusion.refs_0_), channel_id=1, source_target_pairs={{0,32},{8,40},{16,48},{24,56},{32,0},{40,8},{48,16},{56,24},{64,96... | collective-permute-start | bytes 393224 | tf_op jit(solution)/shard_map/ppermute | solution.py:228
  23.0 0.0 collective-permute-start.4
  23.0 2.6 %collective-permute-start.3 = (bf16[4,128,128]{2,1,0:T(8,128)(2,1)S(1)}, bf16[4,128,128]{2,1,0:T(8,128)(2,1)S(1)}, u32[]{:S(2)}, u32[]{:S(2)}) collective-permute-start(bf16[4,128,128]{2,1,0:T(8,128)(2,1)S(1)} %pad_maximum_fusion.refs_0_), channel_id=1, source_target_pairs={{0,16},{8,24},{16,0},{24,8},{32,48},{40,56},{48,32},{56,40},{64,80... | collective-permute-start | bytes 393224 | tf_op jit(solution)/shard_map/ppermute | solution.py:228
  25.6 0.9 %broadcast_multiply_fusion.own_ref = f32[256,128]{1,0:T(8,128)S(1)} fusion(f32[256,128]{1,0:T(8,128)} %get-tuple-element.14), kind=kLoop, calls=%fused_computation.1 | loop fusion | flops 32768 | bytes 262144 | tf_op jit(solution)/shard_map/mul | solution.py:245
  26.5 3.4 %all-to-all-done.parts_ref = bf16[8,256,128]{2,1,0:T(8,128)(2,1)S(1)} async-done(((bf16[8,256,128]{2,1,0:T(8,128)(2,1)}), bf16[8,256,128]{2,1,0:T(8,128)(2,1)S(1)}, u32[]{:S(2)}, u32[]{:S(2)}) %all-to-all-start) | async-done | bytes 524320 | tf_op jit(solution)/shard_map/all_to_all | solution.py:243
  29.9 1.1 %sketch.1 = f32[8,32,128]{2,1,0:T(8,128)} custom-call(bf16[8,256,128]{2,1,0:T(8,128)(2,1)S(1)} %all-to-all-done.parts_ref, f32[256,128]{1,0:T(8,128)S(1)} %broadcast_multiply_fusion.own_ref), custom_call_target="tpu_custom_call" | custom-call | flops 50331648 | bytes 524288 | tf_op jit(solution)/shard_map/sketch/pallas_call | solution.py:172
  31.0 3.4 %all-to-all-start.1 = ((f32[8,32,128]{2,1,0:T(8,128)}), f32[8,32,128]{2,1,0:T(8,128)S(1)}, u32[]{:S(2)}, u32[]{:S(2)}) async-start(f32[8,32,128]{2,1,0:T(8,128)} %sketch.1), calls=%async_computation.1 | async-start | bytes 262144 | tf_op jit(solution)/shard_map/all_to_all | solution.py:246
  34.4 0.1 collective-permute-start.6
  34.5 0.0 collective-permute-done.5.refs_3_
  34.5 0.5 %collective-permute-start.9 = (bf16[4,128,128]{2,1,0:T(8,128)(2,1)S(1)}, bf16[4,128,128]{2,1,0:T(8,128)(2,1)S(1)}, u32[]{:S(2)}, u32[]{:S(2)}) collective-permute-start(bf16[4,128,128]{2,1,0:T(8,128)(2,1)S(1)} %collective-permute-done.5.refs_3_), channel_id=1, source_target_pairs={{0,8},{8,0},{16,24},{24,16},{32,40},{40,32},{48,56},{56,48},{64,72... | collective-permute-start | bytes 393224 | tf_op jit(solution)/shard_map/ppermute | solution.py:228
  35.0 0.0 collective-permute-done.4.refs_2_
  35.0 0.1 collective-permute-start.8
  35.1 0.0 collective-permute-done.3.refs_1_
  35.1 0.4 collective-permute-start.7
  35.5 0.3 collective-permute-done.6.refs_4_
  35.8 0.2 collective-permute-done.9.refs_7_
  36.0 0.3 collective-permute-done.8.refs_6_
  36.3 0.2 collective-permute-done.7.refs_5_
  36.5 4.4 %all-to-all-done.1.sketch_ref = f32[8,32,128]{2,1,0:T(8,128)S(1)} async-done(((f32[8,32,128]{2,1,0:T(8,128)}), f32[8,32,128]{2,1,0:T(8,128)S(1)}, u32[]{:S(2)}, u32[]{:S(2)}) %all-to-all-start.1) | async-done | bytes 131104 | tf_op jit(solution)/shard_map/all_to_all | solution.py:246
  40.9 1.3 %scores.1 = f32[8,128]{1,0:T(8,128)} custom-call(f32[8,32,128]{2,1,0:T(8,128)S(1)} %all-to-all-done.1.sketch_ref, bf16[4,128,128]{2,1,0:T(8,128)(2,1)S(1)} %pad_maximum_fusion.refs_0_, bf16[4,128,128]{2,1,0:T(8,128)(2,1)S(1)} %collective-permute-done.3.refs_1_, bf16[4,128,128]{2,1,0:T(8,128)(2,1)S(1)} %collective-permute-done.4.refs_2_, ...), custom_call_target="tpu_custom_call" | custom-call | tf_op jit(solution)/shard_map/scores/pallas_call | solution.py:208
  (1 shorter events, 0.0 us)
Async XLA Ops:
  0.0 20.7 %copy-start = (bf16[128,128]{1,0:T(8,128)(2,1)S(1)}, bf16[128,128]{1,0:T(8,128)(2,1)}, u32[]{:S(2)}) copy-start(bf16[128,128]{1,0:T(8,128)(2,1)} %param.13) | copy-start | bytes 98308
  0.0 15.8 %collective-permute-start.1 = (bf16[128,128]{1,0:T(8,128)(2,1)}, bf16[128,128]{1,0:T(8,128)(2,1)S(1)}, u32[]{:S(2)}, u32[]{:S(2)}) collective-permute-start(bf16[128,128]{1,0:T(8,128)(2,1)} %param.13), channel_id=1, source_target_pairs={{0,192},{8,200},{16,208},{24,216},{32,224},{40,232},{48,240},{56,2... | collective-permute-start | bytes 98312 | tf_op jit(solution)/shard_map/ppermute | solution.py:228
  6.3 9.5 %collective-permute-start = (bf16[128,128]{1,0:T(8,128)(2,1)}, bf16[128,128]{1,0:T(8,128)(2,1)S(1)}, u32[]{:S(2)}, u32[]{:S(2)}) collective-permute-start(bf16[128,128]{1,0:T(8,128)(2,1)} %param.13), channel_id=1, source_target_pairs={{0,64},{8,72},{16,80},{24,88},{32,96},{40,104},{48,112},{56,120},{... | collective-permute-start | bytes 98312 | tf_op jit(solution)/shard_map/ppermute | solution.py:228
  7.8 8.0 %collective-permute-start.2 = (bf16[128,128]{1,0:T(8,128)(2,1)}, bf16[128,128]{1,0:T(8,128)(2,1)S(1)}, u32[]{:S(2)}, u32[]{:S(2)}) collective-permute-start(bf16[128,128]{1,0:T(8,128)(2,1)} %param.13), channel_id=1, source_target_pairs={{0,128},{8,136},{16,144},{24,152},{32,160},{40,168},{48,176},{56,1... | collective-permute-start | bytes 98312 | tf_op jit(solution)/shard_map/ppermute | solution.py:228
  15.8 14.0 %all-to-all-start = ((bf16[8,256,128]{2,1,0:T(8,128)(2,1)}), bf16[8,256,128]{2,1,0:T(8,128)(2,1)S(1)}, u32[]{:S(2)}, u32[]{:S(2)}) async-start(bf16[8,256,128]{2,1,0:T(8,128)(2,1)} %get-tuple-element.13), calls=%async_computation | async-start | bytes 1048576 | tf_op jit(solution)/shard_map/all_to_all | solution.py:243
  20.8 13.7 %collective-permute-start.5 = (bf16[4,128,128]{2,1,0:T(8,128)(2,1)S(1)}, bf16[4,128,128]{2,1,0:T(8,128)(2,1)S(1)}, u32[]{:S(2)}, u32[]{:S(2)}) collective-permute-start(bf16[4,128,128]{2,1,0:T(8,128)(2,1)S(1)} %pad_maximum_fusion.refs_0_), channel_id=1, source_target_pairs={{0,32},{8,40},{16,48},{24,56},{32,0},{40,8},{48,16},{56,24},{64,96... | collective-permute-start | bytes 393224 | tf_op jit(solution)/shard_map/ppermute | solution.py:228
  23.0 12.0 %collective-permute-start.4 = (bf16[4,128,128]{2,1,0:T(8,128)(2,1)S(1)}, bf16[4,128,128]{2,1,0:T(8,128)(2,1)S(1)}, u32[]{:S(2)}, u32[]{:S(2)}) collective-permute-start(bf16[4,128,128]{2,1,0:T(8,128)(2,1)S(1)} %pad_maximum_fusion.refs_0_), channel_id=1, source_target_pairs={{0,48},{8,56},{16,32},{24,40},{32,16},{40,24},{48,0},{56,8},{64,11... | collective-permute-start | bytes 393224 | tf_op jit(solution)/shard_map/ppermute | solution.py:228
  23.0 12.1 %collective-permute-start.3 = (bf16[4,128,128]{2,1,0:T(8,128)(2,1)S(1)}, bf16[4,128,128]{2,1,0:T(8,128)(2,1)S(1)}, u32[]{:S(2)}, u32[]{:S(2)}) collective-permute-start(bf16[4,128,128]{2,1,0:T(8,128)(2,1)S(1)} %pad_maximum_fusion.refs_0_), channel_id=1, source_target_pairs={{0,16},{8,24},{16,0},{24,8},{32,48},{40,56},{48,32},{56,40},{64,80... | collective-permute-start | bytes 393224 | tf_op jit(solution)/shard_map/ppermute | solution.py:228
  31.0 9.9 %all-to-all-start.1 = ((f32[8,32,128]{2,1,0:T(8,128)}), f32[8,32,128]{2,1,0:T(8,128)S(1)}, u32[]{:S(2)}, u32[]{:S(2)}) async-start(f32[8,32,128]{2,1,0:T(8,128)} %sketch.1), calls=%async_computation.1 | async-start | bytes 262144 | tf_op jit(solution)/shard_map/all_to_all | solution.py:246
  34.4 1.4 %collective-permute-start.6 = (bf16[4,128,128]{2,1,0:T(8,128)(2,1)S(1)}, bf16[4,128,128]{2,1,0:T(8,128)(2,1)S(1)}, u32[]{:S(2)}, u32[]{:S(2)}) collective-permute-start(bf16[4,128,128]{2,1,0:T(8,128)(2,1)S(1)} %pad_maximum_fusion.refs_0_), channel_id=1, source_target_pairs={{0,8},{8,0},{16,24},{24,16},{32,40},{40,32},{48,56},{56,48},{64,72... | collective-permute-start | bytes 393224 | tf_op jit(solution)/shard_map/ppermute | solution.py:228
  34.5 1.5 %collective-permute-start.9 = (bf16[4,128,128]{2,1,0:T(8,128)(2,1)S(1)}, bf16[4,128,128]{2,1,0:T(8,128)(2,1)S(1)}, u32[]{:S(2)}, u32[]{:S(2)}) collective-permute-start(bf16[4,128,128]{2,1,0:T(8,128)(2,1)S(1)} %collective-permute-done.5.refs_3_), channel_id=1, source_target_pairs={{0,8},{8,0},{16,24},{24,16},{32,40},{40,32},{48,56},{56,48},{64,72... | collective-permute-start | bytes 393224 | tf_op jit(solution)/shard_map/ppermute | solution.py:228
  35.0 1.3 %collective-permute-start.8 = (bf16[4,128,128]{2,1,0:T(8,128)(2,1)S(1)}, bf16[4,128,128]{2,1,0:T(8,128)(2,1)S(1)}, u32[]{:S(2)}, u32[]{:S(2)}) collective-permute-start(bf16[4,128,128]{2,1,0:T(8,128)(2,1)S(1)} %collective-permute-done.4.refs_2_), channel_id=1, source_target_pairs={{0,8},{8,0},{16,24},{24,16},{32,40},{40,32},{48,56},{56,48},{64,72... | collective-permute-start | bytes 393224 | tf_op jit(solution)/shard_map/ppermute | solution.py:228
  35.1 1.4 %collective-permute-start.7 = (bf16[4,128,128]{2,1,0:T(8,128)(2,1)S(1)}, bf16[4,128,128]{2,1,0:T(8,128)(2,1)S(1)}, u32[]{:S(2)}, u32[]{:S(2)}) collective-permute-start(bf16[4,128,128]{2,1,0:T(8,128)(2,1)S(1)} %collective-permute-done.3.refs_1_), channel_id=1, source_target_pairs={{0,8},{8,0},{16,24},{24,16},{32,40},{40,32},{48,56},{56,48},{64,72... | collective-permute-start | bytes 393224 | tf_op jit(solution)/shard_map/ppermute | solution.py:228

commit v3 on v2

--- a/solution.py
+++ b/solution.py
@@ -11,7 +11,7 @@
 HB = 256
 F32, BF16, I32 = jnp.float32, jnp.bfloat16, jnp.int32
 MIB = 1024 * 1024
-AHEAD = 3
+PER = 4
 VMEM = functools.partial(pl.BlockSpec, memory_space=pltpu.VMEM)
 HBM = functools.partial(pl.BlockSpec, memory_space=pltpu.HBM)
 
@@ -22,48 +22,20 @@
     return jnp.bitwise_and(value, 1)
 
 
-def terms_kernel(parts, act_hbm, grad_hbm, sign_in_hbm, sign_out_hbm, pick_in_hbm, pick_out_hbm, term_hbm, own_hbm,
-                 act, grad, term, own, sign_in, sign_out, pick_in, pick_out, mat_in, mat_out, sems, send_sems, small_sems):
+def terms_kernel(parts, act, grad, sign_in, sign_out, pick_in, pick_out, from_in, from_out, term_hbm, own_hbm,
+                 term, own, mat_in, mat_out, send_sems):
     examples = act.shape[0]
     picks = pick_in.shape[0]
     cols = 2 * picks
-    small = [
-        pltpu.make_async_copy(source, target, small_sems.at[i])
-        for i, (source, target) in enumerate(
-            (
-                (pick_in_hbm, pick_in),
-                (pick_out_hbm, pick_out),
-                (sign_in_hbm, sign_in),
-                (sign_out_hbm, sign_out),
-            )
-        )
-    ]
-    for copy in small:
-        copy.start()
-    copies = []
-    for e in range(examples):
-        pair = (
-            pltpu.make_async_copy(act_hbm.at[e], act.at[e], sems.at[e, 0]),
-            pltpu.make_async_copy(grad_hbm.at[e], grad.at[e], sems.at[e, 1]),
-        )
-        if e < AHEAD:
-            for copy in pair:
-                copy.start()
-        copies.append(pair)
-
-    for copy in small:
-        copy.wait()
+
+    def send(e):
+        return pltpu.make_async_copy(term.at[e], term_hbm.at[e], send_sems.at[e])
+
     me = lax.axis_index("tensor")
-    row = lax.broadcasted_iota(I32, (cols, picks), 0)
-    lane = lax.broadcasted_iota(I32, (cols, picks), 1)
-    half = picks // 2
-    after = row - picks
-    from_out = jnp.where(after < half, 2 * after, 2 * (after - half) + 1)
+    spread = from_in[...] * pick_in[...].reshape(1, picks).astype(F32)
+    spread = spread + from_out[...] * pick_out[...].reshape(1, picks).astype(F32)
+    pick = jnp.sum(spread, axis=1, keepdims=True).astype(I32)
     zero = jnp.zeros((), F32)
-    spread = jnp.where(row == lane, pick_in[...].reshape(1, picks).astype(F32), zero) + jnp.where(
-        (after >= 0) & (from_out == lane), pick_out[...].reshape(1, picks).astype(F32), zero
-    )
-    pick = jnp.sum(spread, axis=1, keepdims=True).astype(I32)
     is_in = lax.broadcasted_iota(I32, (cols, 1), 0) < picks
 
     def part_of(width):
@@ -87,32 +59,46 @@
         for j in range(matrix.shape[0] // HB):
             span = slice(j * HB, (j + 1) * HB)
             flips = (2 * signs[span].reshape(1, HB) - 1).astype(F32)
-            matrix[span, :] = jnp.where(blocks == j, hadamard * flips, zero).T.astype(BF16)
-
-    sends = []
+            matrix[span, :cols] = jnp.where(blocks == j, hadamard * flips, zero).T.astype(BF16)
+            matrix[span, cols:] = jnp.zeros((HB, matrix.shape[1] - cols), BF16)
+
+
+    tokens = act.shape[1]
+
+    def multiply(*totals):
+        staged = 0
+        for first in range(0, examples, 2 * PER):
+            for matrix, source in ((mat_in, act), (mat_out, grad)):
+                for j in range(matrix.shape[0] // HB):
+                    span = slice(j * HB, (j + 1) * HB)
+                    for unit in range(2):
+                        at = first + unit * PER
+                        pltpu.matmul_push_rhs(matrix[span, :], staged, unit)
+                        left = source[at : at + PER, :, span].reshape(PER * tokens, HB)
+                        pltpu.matmul_acc_lhs(totals[unit], left, load_staged_rhs=staged)
+                    staged = 1 - staged
+            for unit in range(2):
+                whole = pltpu.matmul_pop(totals[unit])
+                for i in range(PER):
+                    e = first + unit * PER + i
+                    part = whole[i * tokens : (i + 1) * tokens, :cols]
+                    term[e] = part.astype(BF16)
+                    send(e).start()
+
+                    @pl.when(me == e)
+                    def _():
+                        own[...] = part
+
+    shape = (PER * tokens, HB)
+    pl.run_scoped(multiply, pltpu.ACC(0)(shape, F32), pltpu.ACC(1)(shape, F32))
+    last = pltpu.make_async_copy(own, own_hbm, send_sems.at[examples])
+    last.start()
     for e in range(examples):
-        for copy in copies[e]:
-            copy.wait()
-        if e + AHEAD < examples:
-            for copy in copies[e + AHEAD]:
-                copy.start()
-        total = jnp.dot(act[e], mat_in[...], preferred_element_type=F32)
-        total = total + jnp.dot(grad[e], mat_out[...], preferred_element_type=F32)
-        term[e] = total.astype(BF16)
-        sends.append(pltpu.make_async_copy(term.at[e], term_hbm.at[e], send_sems.at[e]))
-        sends[e].start()
-
-        @pl.when(me == e)
-        def _():
-            own[...] = total
-
-    sends.append(pltpu.make_async_copy(own, own_hbm, send_sems.at[examples]))
-    sends[-1].start()
-    for copy in sends:
-        copy.wait()
-
-
-def terms(parts, activations, out_grads, signs_in, signs_out, picks_in, picks_out):
+        send(e).wait()
+    last.wait()
+
+
+def terms(parts, activations, out_grads, signs_in, signs_out, picks_in, picks_out, from_in, from_out):
     examples, tokens, width_in = activations.shape
     width_out = out_grads.shape[2]
     cols = 2 * picks_in.shape[0]
@@ -122,31 +108,23 @@
             jax.ShapeDtypeStruct((examples, tokens, cols), BF16),
             jax.ShapeDtypeStruct((tokens, cols), F32),
         ),
-        in_specs=[HBM()] * 6,
+        in_specs=[VMEM()] * 8,
         out_specs=(HBM(), HBM()),
         scratch_shapes=[
-            pltpu.VMEM((examples, tokens, width_in), BF16),
-            pltpu.VMEM((examples, tokens, width_out), BF16),
             pltpu.VMEM((examples, tokens, cols), BF16),
             pltpu.VMEM((tokens, cols), F32),
-            pltpu.VMEM(signs_in.shape, I32),
-            pltpu.VMEM(signs_out.shape, I32),
-            pltpu.VMEM(picks_in.shape, I32),
-            pltpu.VMEM(picks_out.shape, I32),
-            pltpu.VMEM((width_in, cols), BF16),
-            pltpu.VMEM((width_out, cols), BF16),
-            pltpu.SemaphoreType.DMA((examples, 2)),
+            pltpu.VMEM((width_in, HB), BF16),
+            pltpu.VMEM((width_out, HB), BF16),
             pltpu.SemaphoreType.DMA((examples + 1,)),
-            pltpu.SemaphoreType.DMA((4,)),
         ],
-        compiler_params=pltpu.CompilerParams(vmem_limit_bytes=63 * MIB),
+        compiler_params=pltpu.CompilerParams(vmem_limit_bytes=32 * MIB),
         cost_estimate=pl.CostEstimate(
             flops=2 * examples * tokens * cols * (width_in + width_out),
             bytes_accessed=2 * examples * tokens * (width_in + width_out),
             transcendentals=0,
         ),
         name="terms",
-    )(activations, out_grads, signs_in, signs_out, picks_in, picks_out)
+    )(activations, out_grads, signs_in, signs_out, picks_in, picks_out, from_in, from_out)
 
 
 def sketch_kernel(scale, parts_ref, own_ref, out_ref):
@@ -156,10 +134,10 @@
         total = total + jnp.where(me == q, 0.0, parts_ref[q].astype(F32))
     total = total + 2.0 * own_ref[...]
     picks = total.shape[1] // 2
+    half = picks // 2
     outer = lax.dot_general(
         total, total, (((0,), (0,)), ((), ())), precision=lax.Precision.HIGHEST, preferred_element_type=F32
     )
-    half = picks // 2
     sketch = scale * jnp.concatenate(
         [outer[picks : picks + half, :picks], outer[picks + half :, :picks]], axis=1
     )
@@ -215,6 +193,29 @@
     )(sketches, *tests)
 
 
+def layout_kernel(from_in, from_out):
+    shape = from_in.shape
+    row = lax.broadcasted_iota(I32, shape, 0)
+    lane = lax.broadcasted_iota(I32, shape, 1)
+    half = shape[1] // 2
+    after = row - shape[1]
+    out = jnp.where(after < half, 2 * after, 2 * (after - half) + 1)
+    from_in[...] = (row == lane).astype(F32)
+    from_out[...] = ((after >= 0) & (out == lane)).astype(F32)
+
+
+def layout(picks):
+    shape = jax.ShapeDtypeStruct((2 * picks, picks), F32)
+    return pl.pallas_call(
+        layout_kernel,
+        out_shape=(shape, shape),
+        out_specs=(VMEM(), VMEM()),
+        compiler_params=pltpu.CompilerParams(vmem_limit_bytes=2 * MIB),
+        cost_estimate=pl.CostEstimate(flops=20_000_000_000, bytes_accessed=0, transcendentals=0),
+        name="layout",
+    )()
+
+
 def flip(at, which):
     pair = lambda value: value + 1 - 2 * (value % 2)
     return (at, pair(at), 3 - at, pair(3 - at))[which]
@@ -232,10 +233,13 @@
     parts = lax.axis_size("tensor")
     tokens = activations.shape[1]
     sizes = (lax.axis_size("dp") // 8, 4, 2)
-    term, own = terms(parts, activations, out_grads, signs_in, signs_out, picks_in, picks_out)
+    from_in, from_out, block = lax.optimization_barrier((*layout(picks_in.shape[0]), test_sketches))
+    term, own = terms(
+        parts, activations, out_grads, signs_in, signs_out, picks_in, picks_out, from_in, from_out
+    )
     n_z, n_x, n_c = sizes
     devices = n_z * n_x * n_c
-    column = [test_sketches] + [swap(test_sketches, n_x * n_c, n_z, k, devices) for k in (1, 2, 3)]
+    column = [block] + [swap(block, n_x * n_c, n_z, k, devices) for k in (1, 2, 3)]
     term, *column = lax.optimization_barrier((term, *column))
     column = jnp.stack(column)
     plane = [column] + [swap(column, n_c, n_x, k, devices) for k in (1, 2, 3)]

time: 42.4 us -> 39.9 us (0.941)
  Pallas kernels: 9.42 us -> 6.2 us
  waiting for transfers between devices: 8.78 us -> 10.1 us
  other arithmetic: 0.93 us -> 0.03 us
  local copies, waits for them, and re-layouts: 0.01 us -> 0.71 us
    pallas_call x1, Pallas kernels: 7.02 us -> 3.8 us  [terms(): pl.pallas_call(functools.partial(terms_kernel, parts), out_shape=(jax.Sha...]
    ppermute x10, waiting for transfers between devices: 1.04 us -> 2.08 us  [swap(): return lax.ppermute(value, 'dp', pairs)]
    mul x1, other arithmetic: 0.91 us -> 0.01 us  [on_device(): spread = sketch(scale, mine, 0.5 * own)]
    unnamed x2 -> x14, local copies, waits for them, and re-layouts: 0.01 us -> 0.71 us
  transfers between devices with their start and end apart: 12 -> 12, of which waited for: 6 -> 7; matrix products, arithmetic and copies ran while one was open for 2% -> 0% of each run, Pallas kernels for 19% -> 12%
where the time goes in v3:
time: 39.9 us; the launch traced here: 39.6 us
  starting transfers between devices  22.5 us (56%)
  waiting for transfers between devices  10.1 us (25%)
  Pallas kernels  6.2 us (16%)
  local copies, waits for them, and re-layouts  0.71 us (2%)
    ppermute x10, starting transfers between devices, swap(): return lax.ppermute(value, 'dp', pairs)  14.5 us
    all_to_all x1, starting transfers between devices, on_device(): mine = lax.all_to_all(term, 'tensor', 0, 0, tiled=True)  4.58 us
    all_to_all x1, waiting for transfers between devices, on_device(): sketches = lax.all_to_all(spread, 'tensor', 0, 0, tiled=True)  4.38 us
    pallas_call x1, Pallas kernels, terms(): pl.pallas_call(functools.partial(terms_kernel, parts), out_shape=(jax.Sha...  3.8 us
    all_to_all x1, waiting for transfers between devices, on_device(): mine = lax.all_to_all(term, 'tensor', 0, 0, tiled=True)  3.62 us
    all_to_all x1, starting transfers between devices, on_device(): sketches = lax.all_to_all(spread, 'tensor', 0, 0, tiled=True)  3.37 us
    ppermute x10, waiting for transfers between devices, swap(): return lax.ppermute(value, 'dp', pairs)  2.08 us
    pallas_call x1, Pallas kernels, scores(): pl.pallas_call(functools.partial(scores_kernel, sizes), out_shape=jax.Sha...  1.27 us
  transfers between devices with their start and end apart: 12, of which 7 were waited for; matrix products, arithmetic and copies ran while one was open for 0% of the time, Pallas kernels for 12%

profile of v3, /device:TPU:2, one launch (start us, length us, event | category | flops | bytes accessed | tf_op | source)
XLA Modules:
  0.0 39.6 jit_solution(18203395820915904300)
XLA Ops:
  0.0 0.0 copy-start.3
  0.0 0.0 copy-start.2
  0.0 0.0 copy-start.1
  0.0 0.0 copy-start
  0.1 0.7 %copy-done.6 = bf16[128,128]{1,0:T(8,128)(2,1)S(1)} copy-done((bf16[128,128]{1,0:T(8,128)(2,1)S(1)}, bf16[128,128]{1,0:T(8,128)(2,1)}, u32[]{:S(2)}) %copy-start.6) | copy-done | bytes 32792
  0.8 7.2 %collective-permute-start.2 = (bf16[128,128]{1,0:T(8,128)(2,1)S(1)}, bf16[128,128]{1,0:T(8,128)(2,1)S(1)}, u32[]{:S(2)}, u32[]{:S(2)}) collective-permute-start(bf16[128,128]{1,0:T(8,128)(2,1)S(1)} %copy-done.6), channel_id=1, source_target_pairs={{0,128},{8,136},{16,144},{24,152},{32,160},{40,168},{48,176},{56,1... | collective-permute-start | bytes 98312 | tf_op jit(solution)/shard_map/ppermute | solution.py:229
  7.9 0.0 collective-permute-start.1
  8.0 1.5 %collective-permute-start = (bf16[128,128]{1,0:T(8,128)(2,1)S(1)}, bf16[128,128]{1,0:T(8,128)(2,1)S(1)}, u32[]{:S(2)}, u32[]{:S(2)}) collective-permute-start(bf16[128,128]{1,0:T(8,128)(2,1)S(1)} %copy-done.6), channel_id=1, source_target_pairs={{0,64},{8,72},{16,80},{24,88},{32,96},{40,104},{48,112},{56,120},{... | collective-permute-start | bytes 98312 | tf_op jit(solution)/shard_map/ppermute | solution.py:229
  9.5 3.8 %terms.1 = (bf16[8,256,128]{2,1,0:T(8,128)(2,1)}, f32[256,128]{1,0:T(8,128)S(1)}) custom-call(bf16[8,256,1792]{2,1,0:T(8,128)(2,1)S(1)} %copy-done, bf16[8,256,512]{2,1,0:T(8,128)(2,1)S(1)} %copy-done.1, s32[1792]{0:T(1024)S(1)} %copy-done.2, s32[512]{0:T(512)S(1)} %copy-done.3, s32[64]{0:T(128)S(1)} %copy-done.4, s32[64]{0:T(128)S(1)} %copy-done.5, ...), custom_call_target="tpu_custom_call" | custom-call | flops 1207959552 | bytes 9437184 | tf_op jit(solution)/shard_map/terms/pallas_call | solution.py:105
  13.3 0.0 collective-permute-done.2
  13.3 1.1 %collective-permute-done.1 = bf16[128,128]{1,0:T(8,128)(2,1)S(1)} collective-permute-done((bf16[128,128]{1,0:T(8,128)(2,1)S(1)}, bf16[128,128]{1,0:T(8,128)(2,1)S(1)}, u32[]{:S(2)}, u32[]{:S(2)}) %collective-permute-start.1) | collective-permute-done | bytes 32800 | tf_op jit(solution)/shard_map/ppermute | solution.py:229
  14.3 0.0 collective-permute-done
  14.3 4.6 %all-to-all-start = ((bf16[8,256,128]{2,1,0:T(8,128)(2,1)}), bf16[8,256,128]{2,1,0:T(8,128)(2,1)S(1)}, u32[]{:S(2)}, u32[]{:S(2)}) async-start(bf16[8,256,128]{2,1,0:T(8,128)(2,1)} %get-tuple-element.23), calls=%async_computation | async-start | bytes 1048576 | tf_op jit(solution)/shard_map/all_to_all | solution.py:247
  18.9 2.2 %collective-permute-start.5 = (bf16[4,128,128]{2,1,0:T(8,128)(2,1)S(1)}, bf16[4,128,128]{2,1,0:T(8,128)(2,1)S(1)}, u32[]{:S(2)}, u32[]{:S(2)}) collective-permute-start(bf16[4,128,128]{2,1,0:T(8,128)(2,1)S(1)} %pad_maximum_fusion.refs_0_), channel_id=1, source_target_pairs={{0,32},{8,40},{16,48},{24,56},{32,0},{40,8},{48,16},{56,24},{64,96... | collective-permute-start | bytes 393224 | tf_op jit(solution)/shard_map/ppermute | solution.py:229
  21.1 0.0 collective-permute-start.4
  21.1 2.6 %collective-permute-start.3 = (bf16[4,128,128]{2,1,0:T(8,128)(2,1)S(1)}, bf16[4,128,128]{2,1,0:T(8,128)(2,1)S(1)}, u32[]{:S(2)}, u32[]{:S(2)}) collective-permute-start(bf16[4,128,128]{2,1,0:T(8,128)(2,1)S(1)} %pad_maximum_fusion.refs_0_), channel_id=1, source_target_pairs={{0,16},{8,24},{16,0},{24,8},{32,48},{40,56},{48,32},{56,40},{64,80... | collective-permute-start | bytes 393224 | tf_op jit(solution)/shard_map/ppermute | solution.py:229
  23.7 3.6 %all-to-all-done.parts_ref = bf16[8,256,128]{2,1,0:T(8,128)(2,1)S(1)} async-done(((bf16[8,256,128]{2,1,0:T(8,128)(2,1)}), bf16[8,256,128]{2,1,0:T(8,128)(2,1)S(1)}, u32[]{:S(2)}, u32[]{:S(2)}) %all-to-all-start) | async-done | bytes 524320 | tf_op jit(solution)/shard_map/all_to_all | solution.py:247
  27.3 1.1 %sketch.1 = f32[8,32,128]{2,1,0:T(8,128)} custom-call(bf16[8,256,128]{2,1,0:T(8,128)(2,1)S(1)} %all-to-all-done.parts_ref, f32[256,128]{1,0:T(8,128)S(1)} %broadcast_multiply_fusion.own_ref), custom_call_target="tpu_custom_call" | custom-call | flops 50331648 | bytes 524288 | tf_op jit(solution)/shard_map/sketch/pallas_call | solution.py:150
  28.5 3.4 %all-to-all-start.1 = ((f32[8,32,128]{2,1,0:T(8,128)}), f32[8,32,128]{2,1,0:T(8,128)S(1)}, u32[]{:S(2)}, u32[]{:S(2)}) async-start(f32[8,32,128]{2,1,0:T(8,128)} %sketch.1), calls=%async_computation.1 | async-start | bytes 262144 | tf_op jit(solution)/shard_map/all_to_all | solution.py:250
  31.8 0.1 collective-permute-start.6
  31.9 0.0 collective-permute-done.5.refs_3_
  32.0 0.5 %collective-permute-start.9 = (bf16[4,128,128]{2,1,0:T(8,128)(2,1)S(1)}, bf16[4,128,128]{2,1,0:T(8,128)(2,1)S(1)}, u32[]{:S(2)}, u32[]{:S(2)}) collective-permute-start(bf16[4,128,128]{2,1,0:T(8,128)(2,1)S(1)} %collective-permute-done.5.refs_3_), channel_id=1, source_target_pairs={{0,8},{8,0},{16,24},{24,16},{32,40},{40,32},{48,56},{56,48},{64,72... | collective-permute-start | bytes 393224 | tf_op jit(solution)/shard_map/ppermute | solution.py:229
  32.4 0.0 collective-permute-done.4.refs_2_
  32.4 0.1 collective-permute-start.8
  32.6 0.0 collective-permute-done.3.refs_1_
  32.6 0.4 %collective-permute-start.7 = (bf16[4,128,128]{2,1,0:T(8,128)(2,1)S(1)}, bf16[4,128,128]{2,1,0:T(8,128)(2,1)S(1)}, u32[]{:S(2)}, u32[]{:S(2)}) collective-permute-start(bf16[4,128,128]{2,1,0:T(8,128)(2,1)S(1)} %collective-permute-done.3.refs_1_), channel_id=1, source_target_pairs={{0,8},{8,0},{16,24},{24,16},{32,40},{40,32},{48,56},{56,48},{64,72... | collective-permute-start | bytes 393224 | tf_op jit(solution)/shard_map/ppermute | solution.py:229
  33.0 0.3 collective-permute-done.6.refs_4_
  33.3 0.2 collective-permute-done.9.refs_7_
  33.5 0.3 collective-permute-done.8.refs_6_
  33.8 0.2 collective-permute-done.7.refs_5_
  34.0 4.4 %all-to-all-done.1.sketch_ref = f32[8,32,128]{2,1,0:T(8,128)S(1)} async-done(((f32[8,32,128]{2,1,0:T(8,128)}), f32[8,32,128]{2,1,0:T(8,128)S(1)}, u32[]{:S(2)}, u32[]{:S(2)}) %all-to-all-start.1) | async-done | bytes 131104 | tf_op jit(solution)/shard_map/all_to_all | solution.py:250
  38.4 1.3 %scores.1 = f32[8,128]{1,0:T(8,128)} custom-call(f32[8,32,128]{2,1,0:T(8,128)S(1)} %all-to-all-done.1.sketch_ref, bf16[4,128,128]{2,1,0:T(8,128)(2,1)S(1)} %pad_maximum_fusion.refs_0_, bf16[4,128,128]{2,1,0:T(8,128)(2,1)S(1)} %collective-permute-done.3.refs_1_, bf16[4,128,128]{2,1,0:T(8,128)(2,1)S(1)} %collective-permute-done.4.refs_2_, ...), custom_call_target="tpu_custom_call" | custom-call | tf_op jit(solution)/shard_map/scores/pallas_call | solution.py:186
  (12 shorter events, 0.1 us)
Async XLA Ops:
  0.0 0.8 %copy-start.6 = (bf16[128,128]{1,0:T(8,128)(2,1)S(1)}, bf16[128,128]{1,0:T(8,128)(2,1)}, u32[]{:S(2)}) copy-start(bf16[128,128]{1,0:T(8,128)(2,1)} %param.13) | copy-start | bytes 98308
  0.0 9.4 %copy-start.5 = (s32[64]{0:T(128)S(1)}, s32[64]{0:T(128)}, u32[]{:S(2)}) copy-start(s32[64]{0:T(128)} %pick_out.1) | copy-start | bytes 772
  0.0 9.4 %copy-start.4 = (s32[64]{0:T(128)S(1)}, s32[64]{0:T(128)}, u32[]{:S(2)}) copy-start(s32[64]{0:T(128)} %pick_in.1) | copy-start | bytes 772
  0.0 9.4 %copy-start.3 = (s32[512]{0:T(512)S(1)}, s32[512]{0:T(512)}, u32[]{:S(2)}) copy-start(s32[512]{0:T(512)} %sign_out.1) | copy-start | bytes 6148
  0.0 9.4 %copy-start.2 = (s32[1792]{0:T(1024)S(1)}, s32[1792]{0:T(1024)}, u32[]{:S(2)}) copy-start(s32[1792]{0:T(1024)} %sign_in.1) | copy-start | bytes 21508
  0.0 9.4 %copy-start.1 = (bf16[8,256,512]{2,1,0:T(8,128)(2,1)S(1)}, bf16[8,256,512]{2,1,0:T(8,128)(2,1)}, u32[]{:S(2)}) copy-start(bf16[8,256,512]{2,1,0:T(8,128)(2,1)} %grad.1) | copy-start | bytes 6291460
  0.0 9.4 %copy-start = (bf16[8,256,1792]{2,1,0:T(8,128)(2,1)S(1)}, bf16[8,256,1792]{2,1,0:T(8,128)(2,1)}, u32[]{:S(2)}) copy-start(bf16[8,256,1792]{2,1,0:T(8,128)(2,1)} %act.1) | copy-start | bytes 22020100
  0.8 12.5 %collective-permute-start.2 = (bf16[128,128]{1,0:T(8,128)(2,1)S(1)}, bf16[128,128]{1,0:T(8,128)(2,1)S(1)}, u32[]{:S(2)}, u32[]{:S(2)}) collective-permute-start(bf16[128,128]{1,0:T(8,128)(2,1)S(1)} %copy-done.6), channel_id=1, source_target_pairs={{0,128},{8,136},{16,144},{24,152},{32,160},{40,168},{48,176},{56,1... | collective-permute-start | bytes 98312 | tf_op jit(solution)/shard_map/ppermute | solution.py:229
  7.9 6.4 %collective-permute-start.1 = (bf16[128,128]{1,0:T(8,128)(2,1)S(1)}, bf16[128,128]{1,0:T(8,128)(2,1)S(1)}, u32[]{:S(2)}, u32[]{:S(2)}) collective-permute-start(bf16[128,128]{1,0:T(8,128)(2,1)S(1)} %copy-done.6), channel_id=1, source_target_pairs={{0,192},{8,200},{16,208},{24,216},{32,224},{40,232},{48,240},{56,2... | collective-permute-start | bytes 98312 | tf_op jit(solution)/shard_map/ppermute | solution.py:229
  8.0 6.4 %collective-permute-start = (bf16[128,128]{1,0:T(8,128)(2,1)S(1)}, bf16[128,128]{1,0:T(8,128)(2,1)S(1)}, u32[]{:S(2)}, u32[]{:S(2)}) collective-permute-start(bf16[128,128]{1,0:T(8,128)(2,1)S(1)} %copy-done.6), channel_id=1, source_target_pairs={{0,64},{8,72},{16,80},{24,88},{32,96},{40,104},{48,112},{56,120},{... | collective-permute-start | bytes 98312 | tf_op jit(solution)/shard_map/ppermute | solution.py:229
  14.3 13.0 %all-to-all-start = ((bf16[8,256,128]{2,1,0:T(8,128)(2,1)}), bf16[8,256,128]{2,1,0:T(8,128)(2,1)S(1)}, u32[]{:S(2)}, u32[]{:S(2)}) async-start(bf16[8,256,128]{2,1,0:T(8,128)(2,1)} %get-tuple-element.23), calls=%async_computation | async-start | bytes 1048576 | tf_op jit(solution)/shard_map/all_to_all | solution.py:247
  18.9 13.0 %collective-permute-start.5 = (bf16[4,128,128]{2,1,0:T(8,128)(2,1)S(1)}, bf16[4,128,128]{2,1,0:T(8,128)(2,1)S(1)}, u32[]{:S(2)}, u32[]{:S(2)}) collective-permute-start(bf16[4,128,128]{2,1,0:T(8,128)(2,1)S(1)} %pad_maximum_fusion.refs_0_), channel_id=1, source_target_pairs={{0,32},{8,40},{16,48},{24,56},{32,0},{40,8},{48,16},{56,24},{64,96... | collective-permute-start | bytes 393224 | tf_op jit(solution)/shard_map/ppermute | solution.py:229
  21.1 11.3 %collective-permute-start.4 = (bf16[4,128,128]{2,1,0:T(8,128)(2,1)S(1)}, bf16[4,128,128]{2,1,0:T(8,128)(2,1)S(1)}, u32[]{:S(2)}, u32[]{:S(2)}) collective-permute-start(bf16[4,128,128]{2,1,0:T(8,128)(2,1)S(1)} %pad_maximum_fusion.refs_0_), channel_id=1, source_target_pairs={{0,48},{8,56},{16,32},{24,40},{32,16},{40,24},{48,0},{56,8},{64,11... | collective-permute-start | bytes 393224 | tf_op jit(solution)/shard_map/ppermute | solution.py:229
  21.1 11.4 %collective-permute-start.3 = (bf16[4,128,128]{2,1,0:T(8,128)(2,1)S(1)}, bf16[4,128,128]{2,1,0:T(8,128)(2,1)S(1)}, u32[]{:S(2)}, u32[]{:S(2)}) collective-permute-start(bf16[4,128,128]{2,1,0:T(8,128)(2,1)S(1)} %pad_maximum_fusion.refs_0_), channel_id=1, source_target_pairs={{0,16},{8,24},{16,0},{24,8},{32,48},{40,56},{48,32},{56,40},{64,80... | collective-permute-start | bytes 393224 | tf_op jit(solution)/shard_map/ppermute | solution.py:229
  28.5 9.9 %all-to-all-start.1 = ((f32[8,32,128]{2,1,0:T(8,128)}), f32[8,32,128]{2,1,0:T(8,128)S(1)}, u32[]{:S(2)}, u32[]{:S(2)}) async-start(f32[8,32,128]{2,1,0:T(8,128)} %sketch.1), calls=%async_computation.1 | async-start | bytes 262144 | tf_op jit(solution)/shard_map/all_to_all | solution.py:250
  31.8 1.4 %collective-permute-start.6 = (bf16[4,128,128]{2,1,0:T(8,128)(2,1)S(1)}, bf16[4,128,128]{2,1,0:T(8,128)(2,1)S(1)}, u32[]{:S(2)}, u32[]{:S(2)}) collective-permute-start(bf16[4,128,128]{2,1,0:T(8,128)(2,1)S(1)} %pad_maximum_fusion.refs_0_), channel_id=1, source_target_pairs={{0,8},{8,0},{16,24},{24,16},{32,40},{40,32},{48,56},{56,48},{64,72... | collective-permute-start | bytes 393224 | tf_op jit(solution)/shard_map/ppermute | solution.py:229
  32.0 1.5 %collective-permute-start.9 = (bf16[4,128,128]{2,1,0:T(8,128)(2,1)S(1)}, bf16[4,128,128]{2,1,0:T(8,128)(2,1)S(1)}, u32[]{:S(2)}, u32[]{:S(2)}) collective-permute-start(bf16[4,128,128]{2,1,0:T(8,128)(2,1)S(1)} %collective-permute-done.5.refs_3_), channel_id=1, source_target_pairs={{0,8},{8,0},{16,24},{24,16},{32,40},{40,32},{48,56},{56,48},{64,72... | collective-permute-start | bytes 393224 | tf_op jit(solution)/shard_map/ppermute | solution.py:229
  32.4 1.3 %collective-permute-start.8 = (bf16[4,128,128]{2,1,0:T(8,128)(2,1)S(1)}, bf16[4,128,128]{2,1,0:T(8,128)(2,1)S(1)}, u32[]{:S(2)}, u32[]{:S(2)}) collective-permute-start(bf16[4,128,128]{2,1,0:T(8,128)(2,1)S(1)} %collective-permute-done.4.refs_2_), channel_id=1, source_target_pairs={{0,8},{8,0},{16,24},{24,16},{32,40},{40,32},{48,56},{56,48},{64,72... | collective-permute-start | bytes 393224 | tf_op jit(solution)/shard_map/ppermute | solution.py:229
  32.6 1.4 %collective-permute-start.7 = (bf16[4,128,128]{2,1,0:T(8,128)(2,1)S(1)}, bf16[4,128,128]{2,1,0:T(8,128)(2,1)S(1)}, u32[]{:S(2)}, u32[]{:S(2)}) collective-permute-start(bf16[4,128,128]{2,1,0:T(8,128)(2,1)S(1)} %collective-permute-done.3.refs_1_), channel_id=1, source_target_pairs={{0,8},{8,0},{16,24},{24,16},{32,40},{40,32},{48,56},{56,48},{64,72... | collective-permute-start | bytes 393224 | tf_op jit(solution)/shard_map/ppermute | solution.py:229

commit v4 on v3

--- a/solution.py
+++ b/solution.py
@@ -132,7 +132,7 @@
     total = jnp.zeros(own_ref.shape, F32)
     for q in range(parts_ref.shape[0]):
         total = total + jnp.where(me == q, 0.0, parts_ref[q].astype(F32))
-    total = total + 2.0 * own_ref[...]
+    total = total + own_ref[...]
     picks = total.shape[1] // 2
     half = picks // 2
     outer = lax.dot_general(
@@ -141,15 +141,16 @@
     sketch = scale * jnp.concatenate(
         [outer[picks : picks + half, :picks], outer[picks + half :, :picks]], axis=1
     )
-    for q in range(out_ref.shape[0]):
-        out_ref[q] = sketch
+    rows = sketch.shape[0]
+    for q in range(parts_ref.shape[0]):
+        out_ref[q * rows : (q + 1) * rows] = sketch
 
 
 def sketch(scale, parts, own):
     count, tokens, cols = parts.shape
     return pl.pallas_call(
         functools.partial(sketch_kernel, scale),
-        out_shape=jax.ShapeDtypeStruct((count, cols // 4, cols), F32),
+        out_shape=jax.ShapeDtypeStruct((count * cols // 4, cols), F32),
         in_specs=[VMEM(), VMEM()],
         out_specs=VMEM(),
         cost_estimate=pl.CostEstimate(
@@ -165,23 +166,26 @@
     n_z, n_x, n_c = sizes
     me = lax.axis_index("dp")
     my_z, my_x, my_c = me // (n_x * n_c), (me // n_c) % n_x, me % n_c
-    examples = sketch_ref.shape[0]
-    total = jnp.zeros((2 * examples, out_ref.shape[1]), F32)
+    examples = out_ref.shape[0]
+    lefts, rights = [], []
     for c in range(n_c):
         for x in range(n_x):
             for z in range(n_z):
                 index = (flip(my_z, z) * n_x + flip(my_x, x)) * n_c + (my_c + c) % n_c
-                left = sketch_ref[:, pl.ds(index, 1), :].reshape(examples, -1)
-                high = left.astype(BF16).astype(F32)
-                both = jnp.concatenate([high, left - high], axis=0).astype(BF16)
-                total = total + lax.dot_general(
-                    both, tests[c * n_x + x][z], (((1,), (1,)), ((), ())), preferred_element_type=F32
-                )
+                lefts.append(sketch_ref[pl.ds(index, examples, stride=sketch_ref.shape[0] // examples), :])
+                rights.append(tests[c * n_x + x][z])
+    total = jnp.zeros((2 * examples, out_ref.shape[1]), F32)
+    for first in range(0, len(lefts), 32):
+        left = jnp.concatenate(lefts[first : first + 32], axis=1)
+        high = left.astype(BF16).astype(F32)
+        both = jnp.concatenate([high, left - high], axis=0).astype(BF16)
+        right = jnp.concatenate(rights[first : first + 32], axis=1)
+        total = total + lax.dot_general(both, right, (((1,), (1,)), ((), ())), preferred_element_type=F32)
     out_ref[...] = total[:examples] + total[examples:]
 
 
 def scores(sizes, sketches, tests):
-    examples = sketches.shape[0]
+    examples = sketches.shape[0] // (sizes[0] * sizes[1] * sizes[2])
     rows = tests[0].shape[1]
     return pl.pallas_call(
         functools.partial(scores_kernel, sizes),
@@ -246,7 +250,7 @@
     tests = plane + [swap(part, 1, n_c, 1, devices) for part in plane]
     mine = lax.all_to_all(term, "tensor", 0, 0, tiled=True)
     scale = 1.0 / (HB * parts) / math.sqrt(tokens)
-    spread = sketch(scale, mine, 0.5 * own)
+    spread = sketch(scale, mine, own)
     sketches = lax.all_to_all(spread, "tensor", 0, 0, tiled=True)
     return scores(sizes, sketches, tests)
 

time: 39.9 us -> 39.6 us (level)
  no operation moved by 1% of the time
where the time goes in v4:
time: 39.6 us; the launch traced here: 39.4 us
  starting transfers between devices  22.5 us (57%)
  waiting for transfers between devices  10.1 us (26%)
  Pallas kernels  5.95 us (15%)
  local copies, waits for them, and re-layouts  0.71 us (2%)
    ppermute x10, starting transfers between devices, swap(): return lax.ppermute(value, 'dp', pairs)  14.5 us
    all_to_all x1, starting transfers between devices, on_device(): mine = lax.all_to_all(term, 'tensor', 0, 0, tiled=True)  4.58 us
    all_to_all x1, waiting for transfers between devices, on_device(): sketches = lax.all_to_all(spread, 'tensor', 0, 0, tiled=True)  4.38 us
    pallas_call x1, Pallas kernels, terms(): pl.pallas_call(functools.partial(terms_kernel, parts), out_shape=(jax.Sha...  3.8 us
    all_to_all x1, waiting for transfers between devices, on_device(): mine = lax.all_to_all(term, 'tensor', 0, 0, tiled=True)  3.63 us
    all_to_all x1, starting transfers between devices, on_device(): sketches = lax.all_to_all(spread, 'tensor', 0, 0, tiled=True)  3.37 us
    ppermute x10, waiting for transfers between devices, swap(): return lax.ppermute(value, 'dp', pairs)  2.08 us
    pallas_call x1, Pallas kernels, sketch(): pl.pallas_call(functools.partial(sketch_kernel, scale), out_shape=jax.Sha...  1.12 us
  transfers between devices with their start and end apart: 12, of which 7 were waited for; matrix products, arithmetic and copies ran while one was open for 0% of the time, Pallas kernels for 12%

profile of v4, /device:TPU:2, one launch (start us, length us, event | category | flops | bytes accessed | tf_op | source)
XLA Modules:
  0.0 39.4 jit_solution(6854253107324816763)
XLA Ops:
  0.0 0.0 copy-start.3
  0.0 0.0 copy-start.2
  0.0 0.0 copy-start.1
  0.1 0.7 %copy-done.6 = bf16[128,128]{1,0:T(8,128)(2,1)S(1)} copy-done((bf16[128,128]{1,0:T(8,128)(2,1)S(1)}, bf16[128,128]{1,0:T(8,128)(2,1)}, u32[]{:S(2)}) %copy-start.6) | copy-done | bytes 32792
  0.8 7.2 %collective-permute-start.2 = (bf16[128,128]{1,0:T(8,128)(2,1)S(1)}, bf16[128,128]{1,0:T(8,128)(2,1)S(1)}, u32[]{:S(2)}, u32[]{:S(2)}) collective-permute-start(bf16[128,128]{1,0:T(8,128)(2,1)S(1)} %copy-done.6), channel_id=1, source_target_pairs={{0,128},{8,136},{16,144},{24,152},{32,160},{40,168},{48,176},{56,1... | collective-permute-start | bytes 98312 | tf_op jit(solution)/shard_map/ppermute | solution.py:233
  7.9 0.0 collective-permute-start.1
  8.0 1.5 %collective-permute-start = (bf16[128,128]{1,0:T(8,128)(2,1)S(1)}, bf16[128,128]{1,0:T(8,128)(2,1)S(1)}, u32[]{:S(2)}, u32[]{:S(2)}) collective-permute-start(bf16[128,128]{1,0:T(8,128)(2,1)S(1)} %copy-done.6), channel_id=1, source_target_pairs={{0,64},{8,72},{16,80},{24,88},{32,96},{40,104},{48,112},{56,120},{... | collective-permute-start | bytes 98312 | tf_op jit(solution)/shard_map/ppermute | solution.py:233
  9.4 0.0 copy-done.3
  9.5 3.8 %terms.1 = (bf16[8,256,128]{2,1,0:T(8,128)(2,1)}, f32[256,128]{1,0:T(8,128)S(1)}) custom-call(bf16[8,256,1792]{2,1,0:T(8,128)(2,1)S(1)} %copy-done, bf16[8,256,512]{2,1,0:T(8,128)(2,1)S(1)} %copy-done.1, s32[1792]{0:T(1024)S(1)} %copy-done.2, s32[512]{0:T(512)S(1)} %copy-done.3, s32[64]{0:T(128)S(1)} %copy-done.4, s32[64]{0:T(128)S(1)} %copy-done.5, ...), custom_call_target="tpu_custom_call" | custom-call | flops 1207959552 | bytes 9437184 | tf_op jit(solution)/shard_map/terms/pallas_call | solution.py:105
  13.3 0.0 collective-permute-done.2
  13.3 1.1 %collective-permute-done.1 = bf16[128,128]{1,0:T(8,128)(2,1)S(1)} collective-permute-done((bf16[128,128]{1,0:T(8,128)(2,1)S(1)}, bf16[128,128]{1,0:T(8,128)(2,1)S(1)}, u32[]{:S(2)}, u32[]{:S(2)}) %collective-permute-start.1) | collective-permute-done | bytes 32800 | tf_op jit(solution)/shard_map/ppermute | solution.py:233
  14.3 0.0 collective-permute-done
  14.3 4.6 %all-to-all-start = ((bf16[8,256,128]{2,1,0:T(8,128)(2,1)}), bf16[8,256,128]{2,1,0:T(8,128)(2,1)S(1)}, u32[]{:S(2)}, u32[]{:S(2)}) async-start(bf16[8,256,128]{2,1,0:T(8,128)(2,1)} %get-tuple-element.23), calls=%async_computation | async-start | bytes 1048576 | tf_op jit(solution)/shard_map/all_to_all | solution.py:251
  18.9 2.2 %collective-permute-start.5 = (bf16[4,128,128]{2,1,0:T(8,128)(2,1)S(1)}, bf16[4,128,128]{2,1,0:T(8,128)(2,1)S(1)}, u32[]{:S(2)}, u32[]{:S(2)}) collective-permute-start(bf16[4,128,128]{2,1,0:T(8,128)(2,1)S(1)} %pad_maximum_fusion.refs_0_), channel_id=1, source_target_pairs={{0,32},{8,40},{16,48},{24,56},{32,0},{40,8},{48,16},{56,24},{64,96... | collective-permute-start | bytes 393224 | tf_op jit(solution)/shard_map/ppermute | solution.py:233
  21.1 0.0 collective-permute-start.4
  21.1 2.6 %collective-permute-start.3 = (bf16[4,128,128]{2,1,0:T(8,128)(2,1)S(1)}, bf16[4,128,128]{2,1,0:T(8,128)(2,1)S(1)}, u32[]{:S(2)}, u32[]{:S(2)}) collective-permute-start(bf16[4,128,128]{2,1,0:T(8,128)(2,1)S(1)} %pad_maximum_fusion.refs_0_), channel_id=1, source_target_pairs={{0,16},{8,24},{16,0},{24,8},{32,48},{40,56},{48,32},{56,40},{64,80... | collective-permute-start | bytes 393224 | tf_op jit(solution)/shard_map/ppermute | solution.py:233
  23.7 3.6 %all-to-all-done.parts_ref = bf16[8,256,128]{2,1,0:T(8,128)(2,1)S(1)} async-done(((bf16[8,256,128]{2,1,0:T(8,128)(2,1)}), bf16[8,256,128]{2,1,0:T(8,128)(2,1)S(1)}, u32[]{:S(2)}, u32[]{:S(2)}) %all-to-all-start) | async-done | bytes 524320 | tf_op jit(solution)/shard_map/all_to_all | solution.py:251
  27.3 1.1 %sketch.1 = f32[256,128]{1,0:T(8,128)} custom-call(bf16[8,256,128]{2,1,0:T(8,128)(2,1)S(1)} %all-to-all-done.parts_ref, f32[256,128]{1,0:T(8,128)S(1)} %get-tuple-element.24.own_ref), custom_call_target="tpu_custom_call" | custom-call | flops 50331648 | bytes 524288 | tf_op jit(solution)/shard_map/sketch/pallas_call | solution.py:151
  28.5 3.4 %all-to-all-start.1 = ((f32[8,32,128]{2,1,0:T(8,128)}), f32[8,32,128]{2,1,0:T(8,128)S(1)}, u32[]{:S(2)}, u32[]{:S(2)}) async-start(f32[8,32,128]{2,1,0:T(8,128)} %bitcast), calls=%async_computation.1 | async-start | bytes 262144 | tf_op jit(solution)/shard_map/all_to_all | solution.py:254
  31.8 0.1 collective-permute-start.6
  31.9 0.0 collective-permute-done.5.refs_3_
  32.0 0.5 %collective-permute-start.9 = (bf16[4,128,128]{2,1,0:T(8,128)(2,1)S(1)}, bf16[4,128,128]{2,1,0:T(8,128)(2,1)S(1)}, u32[]{:S(2)}, u32[]{:S(2)}) collective-permute-start(bf16[4,128,128]{2,1,0:T(8,128)(2,1)S(1)} %collective-permute-done.5.refs_3_), channel_id=1, source_target_pairs={{0,8},{8,0},{16,24},{24,16},{32,40},{40,32},{48,56},{56,48},{64,72... | collective-permute-start | bytes 393224 | tf_op jit(solution)/shard_map/ppermute | solution.py:233
  32.4 0.0 collective-permute-done.4.refs_2_
  32.5 0.1 collective-permute-start.8
  32.6 0.0 collective-permute-done.3.refs_1_
  32.6 0.4 %collective-permute-start.7 = (bf16[4,128,128]{2,1,0:T(8,128)(2,1)S(1)}, bf16[4,128,128]{2,1,0:T(8,128)(2,1)S(1)}, u32[]{:S(2)}, u32[]{:S(2)}) collective-permute-start(bf16[4,128,128]{2,1,0:T(8,128)(2,1)S(1)} %collective-permute-done.3.refs_1_), channel_id=1, source_target_pairs={{0,8},{8,0},{16,24},{24,16},{32,40},{40,32},{48,56},{56,48},{64,72... | collective-permute-start | bytes 393224 | tf_op jit(solution)/shard_map/ppermute | solution.py:233
  33.0 0.3 collective-permute-done.6.refs_4_
  33.3 0.2 collective-permute-done.9.refs_7_
  33.5 0.3 collective-permute-done.8.refs_6_
  33.8 0.2 collective-permute-done.7.refs_5_
  34.0 4.4 %all-to-all-done.1 = f32[8,32,128]{2,1,0:T(8,128)S(1)} async-done(((f32[8,32,128]{2,1,0:T(8,128)}), f32[8,32,128]{2,1,0:T(8,128)S(1)}, u32[]{:S(2)}, u32[]{:S(2)}) %all-to-all-start.1) | async-done | bytes 131104 | tf_op jit(solution)/shard_map/all_to_all | solution.py:254
  38.4 1.0 %scores.1 = f32[8,128]{1,0:T(8,128)} custom-call(f32[256,128]{1,0:T(8,128)S(1)} %bitcast.6, bf16[4,128,128]{2,1,0:T(8,128)(2,1)S(1)} %pad_maximum_fusion.refs_0_, bf16[4,128,128]{2,1,0:T(8,128)(2,1)S(1)} %collective-permute-done.3.refs_1_, bf16[4,128,128]{2,1,0:T(8,128)(2,1)S(1)} %collective-permute-done.4.refs_2_, ...), custom_call_target="tpu_custom_call" | custom-call | tf_op jit(solution)/shard_map/scores/pallas_call | solution.py:190
  (11 shorter events, 0.1 us)
Async XLA Ops:
  0.0 0.8 %copy-start.6 = (bf16[128,128]{1,0:T(8,128)(2,1)S(1)}, bf16[128,128]{1,0:T(8,128)(2,1)}, u32[]{:S(2)}) copy-start(bf16[128,128]{1,0:T(8,128)(2,1)} %param.13) | copy-start | bytes 98308
  0.0 9.4 %copy-start.5 = (s32[64]{0:T(128)S(1)}, s32[64]{0:T(128)}, u32[]{:S(2)}) copy-start(s32[64]{0:T(128)} %pick_out.1) | copy-start | bytes 772
  0.0 9.4 %copy-start.4 = (s32[64]{0:T(128)S(1)}, s32[64]{0:T(128)}, u32[]{:S(2)}) copy-start(s32[64]{0:T(128)} %pick_in.1) | copy-start | bytes 772
  0.0 9.4 %copy-start.3 = (s32[512]{0:T(512)S(1)}, s32[512]{0:T(512)}, u32[]{:S(2)}) copy-start(s32[512]{0:T(512)} %sign_out.1) | copy-start | bytes 6148
  0.0 9.4 %copy-start.2 = (s32[1792]{0:T(1024)S(1)}, s32[1792]{0:T(1024)}, u32[]{:S(2)}) copy-start(s32[1792]{0:T(1024)} %sign_in.1) | copy-start | bytes 21508
  0.0 9.4 %copy-start.1 = (bf16[8,256,512]{2,1,0:T(8,128)(2,1)S(1)}, bf16[8,256,512]{2,1,0:T(8,128)(2,1)}, u32[]{:S(2)}) copy-start(bf16[8,256,512]{2,1,0:T(8,128)(2,1)} %grad.1) | copy-start | bytes 6291460
  0.0 9.4 %copy-start = (bf16[8,256,1792]{2,1,0:T(8,128)(2,1)S(1)}, bf16[8,256,1792]{2,1,0:T(8,128)(2,1)}, u32[]{:S(2)}) copy-start(bf16[8,256,1792]{2,1,0:T(8,128)(2,1)} %act.1) | copy-start | bytes 22020100
  0.8 12.5 %collective-permute-start.2 = (bf16[128,128]{1,0:T(8,128)(2,1)S(1)}, bf16[128,128]{1,0:T(8,128)(2,1)S(1)}, u32[]{:S(2)}, u32[]{:S(2)}) collective-permute-start(bf16[128,128]{1,0:T(8,128)(2,1)S(1)} %copy-done.6), channel_id=1, source_target_pairs={{0,128},{8,136},{16,144},{24,152},{32,160},{40,168},{48,176},{56,1... | collective-permute-start | bytes 98312 | tf_op jit(solution)/shard_map/ppermute | solution.py:233
  7.9 6.4 %collective-permute-start.1 = (bf16[128,128]{1,0:T(8,128)(2,1)S(1)}, bf16[128,128]{1,0:T(8,128)(2,1)S(1)}, u32[]{:S(2)}, u32[]{:S(2)}) collective-permute-start(bf16[128,128]{1,0:T(8,128)(2,1)S(1)} %copy-done.6), channel_id=1, source_target_pairs={{0,192},{8,200},{16,208},{24,216},{32,224},{40,232},{48,240},{56,2... | collective-permute-start | bytes 98312 | tf_op jit(solution)/shard_map/ppermute | solution.py:233
  8.0 6.4 %collective-permute-start = (bf16[128,128]{1,0:T(8,128)(2,1)S(1)}, bf16[128,128]{1,0:T(8,128)(2,1)S(1)}, u32[]{:S(2)}, u32[]{:S(2)}) collective-permute-start(bf16[128,128]{1,0:T(8,128)(2,1)S(1)} %copy-done.6), channel_id=1, source_target_pairs={{0,64},{8,72},{16,80},{24,88},{32,96},{40,104},{48,112},{56,120},{... | collective-permute-start | bytes 98312 | tf_op jit(solution)/shard_map/ppermute | solution.py:233
  14.3 13.0 %all-to-all-start = ((bf16[8,256,128]{2,1,0:T(8,128)(2,1)}), bf16[8,256,128]{2,1,0:T(8,128)(2,1)S(1)}, u32[]{:S(2)}, u32[]{:S(2)}) async-start(bf16[8,256,128]{2,1,0:T(8,128)(2,1)} %get-tuple-element.23), calls=%async_computation | async-start | bytes 1048576 | tf_op jit(solution)/shard_map/all_to_all | solution.py:251
  18.9 13.0 %collective-permute-start.5 = (bf16[4,128,128]{2,1,0:T(8,128)(2,1)S(1)}, bf16[4,128,128]{2,1,0:T(8,128)(2,1)S(1)}, u32[]{:S(2)}, u32[]{:S(2)}) collective-permute-start(bf16[4,128,128]{2,1,0:T(8,128)(2,1)S(1)} %pad_maximum_fusion.refs_0_), channel_id=1, source_target_pairs={{0,32},{8,40},{16,48},{24,56},{32,0},{40,8},{48,16},{56,24},{64,96... | collective-permute-start | bytes 393224 | tf_op jit(solution)/shard_map/ppermute | solution.py:233
  21.1 11.3 %collective-permute-start.4 = (bf16[4,128,128]{2,1,0:T(8,128)(2,1)S(1)}, bf16[4,128,128]{2,1,0:T(8,128)(2,1)S(1)}, u32[]{:S(2)}, u32[]{:S(2)}) collective-permute-start(bf16[4,128,128]{2,1,0:T(8,128)(2,1)S(1)} %pad_maximum_fusion.refs_0_), channel_id=1, source_target_pairs={{0,48},{8,56},{16,32},{24,40},{32,16},{40,24},{48,0},{56,8},{64,11... | collective-permute-start | bytes 393224 | tf_op jit(solution)/shard_map/ppermute | solution.py:233
  21.1 11.4 %collective-permute-start.3 = (bf16[4,128,128]{2,1,0:T(8,128)(2,1)S(1)}, bf16[4,128,128]{2,1,0:T(8,128)(2,1)S(1)}, u32[]{:S(2)}, u32[]{:S(2)}) collective-permute-start(bf16[4,128,128]{2,1,0:T(8,128)(2,1)S(1)} %pad_maximum_fusion.refs_0_), channel_id=1, source_target_pairs={{0,16},{8,24},{16,0},{24,8},{32,48},{40,56},{48,32},{56,40},{64,80... | collective-permute-start | bytes 393224 | tf_op jit(solution)/shard_map/ppermute | solution.py:233
  28.5 9.9 %all-to-all-start.1 = ((f32[8,32,128]{2,1,0:T(8,128)}), f32[8,32,128]{2,1,0:T(8,128)S(1)}, u32[]{:S(2)}, u32[]{:S(2)}) async-start(f32[8,32,128]{2,1,0:T(8,128)} %bitcast), calls=%async_computation.1 | async-start | bytes 262144 | tf_op jit(solution)/shard_map/all_to_all | solution.py:254
  31.8 1.4 %collective-permute-start.6 = (bf16[4,128,128]{2,1,0:T(8,128)(2,1)S(1)}, bf16[4,128,128]{2,1,0:T(8,128)(2,1)S(1)}, u32[]{:S(2)}, u32[]{:S(2)}) collective-permute-start(bf16[4,128,128]{2,1,0:T(8,128)(2,1)S(1)} %pad_maximum_fusion.refs_0_), channel_id=1, source_target_pairs={{0,8},{8,0},{16,24},{24,16},{32,40},{40,32},{48,56},{56,48},{64,72... | collective-permute-start | bytes 393224 | tf_op jit(solution)/shard_map/ppermute | solution.py:233
  32.0 1.5 %collective-permute-start.9 = (bf16[4,128,128]{2,1,0:T(8,128)(2,1)S(1)}, bf16[4,128,128]{2,1,0:T(8,128)(2,1)S(1)}, u32[]{:S(2)}, u32[]{:S(2)}) collective-permute-start(bf16[4,128,128]{2,1,0:T(8,128)(2,1)S(1)} %collective-permute-done.5.refs_3_), channel_id=1, source_target_pairs={{0,8},{8,0},{16,24},{24,16},{32,40},{40,32},{48,56},{56,48},{64,72... | collective-permute-start | bytes 393224 | tf_op jit(solution)/shard_map/ppermute | solution.py:233
  32.5 1.3 %collective-permute-start.8 = (bf16[4,128,128]{2,1,0:T(8,128)(2,1)S(1)}, bf16[4,128,128]{2,1,0:T(8,128)(2,1)S(1)}, u32[]{:S(2)}, u32[]{:S(2)}) collective-permute-start(bf16[4,128,128]{2,1,0:T(8,128)(2,1)S(1)} %collective-permute-done.4.refs_2_), channel_id=1, source_target_pairs={{0,8},{8,0},{16,24},{24,16},{32,40},{40,32},{48,56},{56,48},{64,72... | collective-permute-start | bytes 393224 | tf_op jit(solution)/shard_map/ppermute | solution.py:233
  32.6 1.4 %collective-permute-start.7 = (bf16[4,128,128]{2,1,0:T(8,128)(2,1)S(1)}, bf16[4,128,128]{2,1,0:T(8,128)(2,1)S(1)}, u32[]{:S(2)}, u32[]{:S(2)}) collective-permute-start(bf16[4,128,128]{2,1,0:T(8,128)(2,1)S(1)} %collective-permute-done.3.refs_1_), channel_id=1, source_target_pairs={{0,8},{8,0},{16,24},{24,16},{32,40},{40,32},{48,56},{56,48},{64,72... | collective-permute-start | bytes 393224 | tf_op jit(solution)/shard_map/ppermute | solution.py:233

commit v5 on v4

--- a/solution.py
+++ b/solution.py
@@ -243,7 +243,9 @@
     )
     n_z, n_x, n_c = sizes
     devices = n_z * n_x * n_c
-    column = [block] + [swap(block, n_x * n_c, n_z, k, devices) for k in (1, 2, 3)]
+    column = [block] + [
+        swap(test_sketches if k == 3 else block, n_x * n_c, n_z, k, devices) for k in (1, 2, 3)
+    ]
     term, *column = lax.optimization_barrier((term, *column))
     column = jnp.stack(column)
     plane = [column] + [swap(column, n_c, n_x, k, devices) for k in (1, 2, 3)]

time: 39.6 us -> 39.2 us (0.990)
  local copies, waits for them, and re-layouts: 0.71 us -> 0.03 us
    unnamed x14, local copies, waits for them, and re-layouts: 0.71 us -> 0.03 us
  transfers between devices with their start and end apart: 12 -> 12, of which waited for: 7 -> 7; matrix products, arithmetic and copies ran while one was open for 0% -> 0% of each run, Pallas kernels for 12% -> 13%
where the time goes in v5:
time: 39.2 us; the launch traced here: 39 us
  starting transfers between devices  22.8 us (58%)
  waiting for transfers between devices  10.1 us (26%)
  Pallas kernels  5.95 us (15%)
    ppermute x10, starting transfers between devices, swap(): return lax.ppermute(value, 'dp', pairs)  14.8 us
    all_to_all x1, starting transfers between devices, on_device(): mine = lax.all_to_all(term, 'tensor', 0, 0, tiled=True)  4.58 us
    all_to_all x1, waiting for transfers between devices, on_device(): sketches = lax.all_to_all(spread, 'tensor', 0, 0, tiled=True)  4.38 us
    pallas_call x1, Pallas kernels, terms(): pl.pallas_call(functools.partial(terms_kernel, parts), out_shape=(jax.Sha...  3.8 us
    all_to_all x1, waiting for transfers between devices, on_device(): mine = lax.all_to_all(term, 'tensor', 0, 0, tiled=True)  3.73 us
    all_to_all x1, starting transfers between devices, on_device(): sketches = lax.all_to_all(spread, 'tensor', 0, 0, tiled=True)  3.37 us
    ppermute x10, waiting for transfers between devices, swap(): return lax.ppermute(value, 'dp', pairs)  1.99 us
    pallas_call x1, Pallas kernels, sketch(): pl.pallas_call(functools.partial(sketch_kernel, scale), out_shape=jax.Sha...  1.12 us
  transfers between devices with their start and end apart: 12, of which 7 were waited for; matrix products, arithmetic and copies ran while one was open for 0% of the time, Pallas kernels for 13%

profile of v5, /device:TPU:2, one launch (start us, length us, event | category | flops | bytes accessed | tf_op | source)
XLA Modules:
  0.0 39.0 jit_solution(15633229503690851998)
XLA Ops:
  0.0 0.0 copy-start.3
  0.0 0.0 copy-start.2
  0.0 7.3 %collective-permute-start.2 = (bf16[128,128]{1,0:T(8,128)(2,1)}, bf16[128,128]{1,0:T(8,128)(2,1)S(1)}, u32[]{:S(2)}, u32[]{:S(2)}) collective-permute-start(bf16[128,128]{1,0:T(8,128)(2,1)} %param.13), channel_id=1, source_target_pairs={{0,128},{8,136},{16,144},{24,152},{32,160},{40,168},{48,176},{56,1... | collective-permute-start | bytes 98312 | tf_op jit(solution)/shard_map/ppermute | solution.py:233
  7.4 0.1 collective-permute-start.1
  7.5 1.6 %collective-permute-start = (bf16[128,128]{1,0:T(8,128)(2,1)S(1)}, bf16[128,128]{1,0:T(8,128)(2,1)S(1)}, u32[]{:S(2)}, u32[]{:S(2)}) collective-permute-start(bf16[128,128]{1,0:T(8,128)(2,1)S(1)} %copy-done.6), channel_id=1, source_target_pairs={{0,64},{8,72},{16,80},{24,88},{32,96},{40,104},{48,112},{56,120},{... | collective-permute-start | bytes 98312 | tf_op jit(solution)/shard_map/ppermute | solution.py:233
  9.0 0.0 copy-done.2
  9.0 0.0 copy-done.1
  9.0 0.0 copy-done
  9.0 3.8 %terms.1 = (bf16[8,256,128]{2,1,0:T(8,128)(2,1)}, f32[256,128]{1,0:T(8,128)S(1)}) custom-call(bf16[8,256,1792]{2,1,0:T(8,128)(2,1)S(1)} %copy-done, bf16[8,256,512]{2,1,0:T(8,128)(2,1)S(1)} %copy-done.1, s32[1792]{0:T(1024)S(1)} %copy-done.2, s32[512]{0:T(512)S(1)} %copy-done.3, s32[64]{0:T(128)S(1)} %copy-done.4, s32[64]{0:T(128)S(1)} %copy-done.5, ...), custom_call_target="tpu_custom_call" | custom-call | flops 1207959552 | bytes 9437184 | tf_op jit(solution)/shard_map/terms/pallas_call | solution.py:105
  12.9 0.0 collective-permute-done.2
  12.9 1.0 %collective-permute-done.1 = bf16[128,128]{1,0:T(8,128)(2,1)S(1)} collective-permute-done((bf16[128,128]{1,0:T(8,128)(2,1)S(1)}, bf16[128,128]{1,0:T(8,128)(2,1)S(1)}, u32[]{:S(2)}, u32[]{:S(2)}) %collective-permute-start.1) | collective-permute-done | bytes 32800 | tf_op jit(solution)/shard_map/ppermute | solution.py:233
  13.8 0.0 collective-permute-done
  13.8 4.6 %all-to-all-start = ((bf16[8,256,128]{2,1,0:T(8,128)(2,1)}), bf16[8,256,128]{2,1,0:T(8,128)(2,1)S(1)}, u32[]{:S(2)}, u32[]{:S(2)}) async-start(bf16[8,256,128]{2,1,0:T(8,128)(2,1)} %get-tuple-element.23), calls=%async_computation | async-start | bytes 1048576 | tf_op jit(solution)/shard_map/all_to_all | solution.py:253
  18.4 2.2 %collective-permute-start.5 = (bf16[4,128,128]{2,1,0:T(8,128)(2,1)S(1)}, bf16[4,128,128]{2,1,0:T(8,128)(2,1)S(1)}, u32[]{:S(2)}, u32[]{:S(2)}) collective-permute-start(bf16[4,128,128]{2,1,0:T(8,128)(2,1)S(1)} %pad_maximum_fusion.refs_0_), channel_id=1, source_target_pairs={{0,32},{8,40},{16,48},{24,56},{32,0},{40,8},{48,16},{56,24},{64,96... | collective-permute-start | bytes 393224 | tf_op jit(solution)/shard_map/ppermute | solution.py:233
  20.6 0.0 collective-permute-start.4
  20.6 2.6 %collective-permute-start.3 = (bf16[4,128,128]{2,1,0:T(8,128)(2,1)S(1)}, bf16[4,128,128]{2,1,0:T(8,128)(2,1)S(1)}, u32[]{:S(2)}, u32[]{:S(2)}) collective-permute-start(bf16[4,128,128]{2,1,0:T(8,128)(2,1)S(1)} %pad_maximum_fusion.refs_0_), channel_id=1, source_target_pairs={{0,16},{8,24},{16,0},{24,8},{32,48},{40,56},{48,32},{56,40},{64,80... | collective-permute-start | bytes 393224 | tf_op jit(solution)/shard_map/ppermute | solution.py:233
  23.2 3.7 %all-to-all-done.parts_ref = bf16[8,256,128]{2,1,0:T(8,128)(2,1)S(1)} async-done(((bf16[8,256,128]{2,1,0:T(8,128)(2,1)}), bf16[8,256,128]{2,1,0:T(8,128)(2,1)S(1)}, u32[]{:S(2)}, u32[]{:S(2)}) %all-to-all-start) | async-done | bytes 524320 | tf_op jit(solution)/shard_map/all_to_all | solution.py:253
  26.9 1.1 %sketch.1 = f32[256,128]{1,0:T(8,128)} custom-call(bf16[8,256,128]{2,1,0:T(8,128)(2,1)S(1)} %all-to-all-done.parts_ref, f32[256,128]{1,0:T(8,128)S(1)} %get-tuple-element.24.own_ref), custom_call_target="tpu_custom_call" | custom-call | flops 50331648 | bytes 524288 | tf_op jit(solution)/shard_map/sketch/pallas_call | solution.py:151
  28.1 3.4 %all-to-all-start.1 = ((f32[8,32,128]{2,1,0:T(8,128)}), f32[8,32,128]{2,1,0:T(8,128)S(1)}, u32[]{:S(2)}, u32[]{:S(2)}) async-start(f32[8,32,128]{2,1,0:T(8,128)} %bitcast), calls=%async_computation.1 | async-start | bytes 262144 | tf_op jit(solution)/shard_map/all_to_all | solution.py:256
  31.4 0.1 collective-permute-start.6
  31.5 0.0 collective-permute-done.5.refs_3_
  31.5 0.5 %collective-permute-start.9 = (bf16[4,128,128]{2,1,0:T(8,128)(2,1)S(1)}, bf16[4,128,128]{2,1,0:T(8,128)(2,1)S(1)}, u32[]{:S(2)}, u32[]{:S(2)}) collective-permute-start(bf16[4,128,128]{2,1,0:T(8,128)(2,1)S(1)} %collective-permute-done.5.refs_3_), channel_id=1, source_target_pairs={{0,8},{8,0},{16,24},{24,16},{32,40},{40,32},{48,56},{56,48},{64,72... | collective-permute-start | bytes 393224 | tf_op jit(solution)/shard_map/ppermute | solution.py:233
  32.0 0.0 collective-permute-done.4.refs_2_
  32.0 0.1 collective-permute-start.8
  32.1 0.0 collective-permute-done.3.refs_1_
  32.2 0.4 %collective-permute-start.7 = (bf16[4,128,128]{2,1,0:T(8,128)(2,1)S(1)}, bf16[4,128,128]{2,1,0:T(8,128)(2,1)S(1)}, u32[]{:S(2)}, u32[]{:S(2)}) collective-permute-start(bf16[4,128,128]{2,1,0:T(8,128)(2,1)S(1)} %collective-permute-done.3.refs_1_), channel_id=1, source_target_pairs={{0,8},{8,0},{16,24},{24,16},{32,40},{40,32},{48,56},{56,48},{64,72... | collective-permute-start | bytes 393224 | tf_op jit(solution)/shard_map/ppermute | solution.py:233
  32.6 0.3 collective-permute-done.6.refs_4_
  32.9 0.2 collective-permute-done.9.refs_7_
  33.1 0.3 collective-permute-done.8.refs_6_
  33.4 0.2 collective-permute-done.7.refs_5_
  33.6 4.4 %all-to-all-done.1 = f32[8,32,128]{2,1,0:T(8,128)S(1)} async-done(((f32[8,32,128]{2,1,0:T(8,128)}), f32[8,32,128]{2,1,0:T(8,128)S(1)}, u32[]{:S(2)}, u32[]{:S(2)}) %all-to-all-start.1) | async-done | bytes 131104 | tf_op jit(solution)/shard_map/all_to_all | solution.py:256
  38.0 1.0 %scores.1 = f32[8,128]{1,0:T(8,128)} custom-call(f32[256,128]{1,0:T(8,128)S(1)} %bitcast.6, bf16[4,128,128]{2,1,0:T(8,128)(2,1)S(1)} %pad_maximum_fusion.refs_0_, bf16[4,128,128]{2,1,0:T(8,128)(2,1)S(1)} %collective-permute-done.3.refs_1_, bf16[4,128,128]{2,1,0:T(8,128)(2,1)S(1)} %collective-permute-done.4.refs_2_, ...), custom_call_target="tpu_custom_call" | custom-call | tf_op jit(solution)/shard_map/scores/pallas_call | solution.py:190
  (11 shorter events, 0.1 us)
Async XLA Ops:
  0.0 7.3 %copy-start.6 = (bf16[128,128]{1,0:T(8,128)(2,1)S(1)}, bf16[128,128]{1,0:T(8,128)(2,1)}, u32[]{:S(2)}) copy-start(bf16[128,128]{1,0:T(8,128)(2,1)} %param.13) | copy-start | bytes 98308
  0.0 9.0 %copy-start.5 = (s32[64]{0:T(128)S(1)}, s32[64]{0:T(128)}, u32[]{:S(2)}) copy-start(s32[64]{0:T(128)} %pick_out.1) | copy-start | bytes 772
  0.0 9.0 %copy-start.4 = (s32[64]{0:T(128)S(1)}, s32[64]{0:T(128)}, u32[]{:S(2)}) copy-start(s32[64]{0:T(128)} %pick_in.1) | copy-start | bytes 772
  0.0 9.0 %copy-start.3 = (s32[512]{0:T(512)S(1)}, s32[512]{0:T(512)}, u32[]{:S(2)}) copy-start(s32[512]{0:T(512)} %sign_out.1) | copy-start | bytes 6148
  0.0 9.0 %copy-start.2 = (s32[1792]{0:T(1024)S(1)}, s32[1792]{0:T(1024)}, u32[]{:S(2)}) copy-start(s32[1792]{0:T(1024)} %sign_in.1) | copy-start | bytes 21508
  0.0 9.0 %copy-start.1 = (bf16[8,256,512]{2,1,0:T(8,128)(2,1)S(1)}, bf16[8,256,512]{2,1,0:T(8,128)(2,1)}, u32[]{:S(2)}) copy-start(bf16[8,256,512]{2,1,0:T(8,128)(2,1)} %grad.1) | copy-start | bytes 6291460
  0.0 9.0 %copy-start = (bf16[8,256,1792]{2,1,0:T(8,128)(2,1)S(1)}, bf16[8,256,1792]{2,1,0:T(8,128)(2,1)}, u32[]{:S(2)}) copy-start(bf16[8,256,1792]{2,1,0:T(8,128)(2,1)} %act.1) | copy-start | bytes 22020100
  0.0 12.8 %collective-permute-start.2 = (bf16[128,128]{1,0:T(8,128)(2,1)}, bf16[128,128]{1,0:T(8,128)(2,1)S(1)}, u32[]{:S(2)}, u32[]{:S(2)}) collective-permute-start(bf16[128,128]{1,0:T(8,128)(2,1)} %param.13), channel_id=1, source_target_pairs={{0,128},{8,136},{16,144},{24,152},{32,160},{40,168},{48,176},{56,1... | collective-permute-start | bytes 98312 | tf_op jit(solution)/shard_map/ppermute | solution.py:233
  7.4 6.5 %collective-permute-start.1 = (bf16[128,128]{1,0:T(8,128)(2,1)S(1)}, bf16[128,128]{1,0:T(8,128)(2,1)S(1)}, u32[]{:S(2)}, u32[]{:S(2)}) collective-permute-start(bf16[128,128]{1,0:T(8,128)(2,1)S(1)} %copy-done.6), channel_id=1, source_target_pairs={{0,192},{8,200},{16,208},{24,216},{32,224},{40,232},{48,240},{56,2... | collective-permute-start | bytes 98312 | tf_op jit(solution)/shard_map/ppermute | solution.py:233
  7.5 6.4 %collective-permute-start = (bf16[128,128]{1,0:T(8,128)(2,1)S(1)}, bf16[128,128]{1,0:T(8,128)(2,1)S(1)}, u32[]{:S(2)}, u32[]{:S(2)}) collective-permute-start(bf16[128,128]{1,0:T(8,128)(2,1)S(1)} %copy-done.6), channel_id=1, source_target_pairs={{0,64},{8,72},{16,80},{24,88},{32,96},{40,104},{48,112},{56,120},{... | collective-permute-start | bytes 98312 | tf_op jit(solution)/shard_map/ppermute | solution.py:233
  13.8 13.1 %all-to-all-start = ((bf16[8,256,128]{2,1,0:T(8,128)(2,1)}), bf16[8,256,128]{2,1,0:T(8,128)(2,1)S(1)}, u32[]{:S(2)}, u32[]{:S(2)}) async-start(bf16[8,256,128]{2,1,0:T(8,128)(2,1)} %get-tuple-element.23), calls=%async_computation | async-start | bytes 1048576 | tf_op jit(solution)/shard_map/all_to_all | solution.py:253
  18.4 13.1 %collective-permute-start.5 = (bf16[4,128,128]{2,1,0:T(8,128)(2,1)S(1)}, bf16[4,128,128]{2,1,0:T(8,128)(2,1)S(1)}, u32[]{:S(2)}, u32[]{:S(2)}) collective-permute-start(bf16[4,128,128]{2,1,0:T(8,128)(2,1)S(1)} %pad_maximum_fusion.refs_0_), channel_id=1, source_target_pairs={{0,32},{8,40},{16,48},{24,56},{32,0},{40,8},{48,16},{56,24},{64,96... | collective-permute-start | bytes 393224 | tf_op jit(solution)/shard_map/ppermute | solution.py:233
  20.6 11.4 %collective-permute-start.4 = (bf16[4,128,128]{2,1,0:T(8,128)(2,1)S(1)}, bf16[4,128,128]{2,1,0:T(8,128)(2,1)S(1)}, u32[]{:S(2)}, u32[]{:S(2)}) collective-permute-start(bf16[4,128,128]{2,1,0:T(8,128)(2,1)S(1)} %pad_maximum_fusion.refs_0_), channel_id=1, source_target_pairs={{0,48},{8,56},{16,32},{24,40},{32,16},{40,24},{48,0},{56,8},{64,11... | collective-permute-start | bytes 393224 | tf_op jit(solution)/shard_map/ppermute | solution.py:233
  20.6 11.5 %collective-permute-start.3 = (bf16[4,128,128]{2,1,0:T(8,128)(2,1)S(1)}, bf16[4,128,128]{2,1,0:T(8,128)(2,1)S(1)}, u32[]{:S(2)}, u32[]{:S(2)}) collective-permute-start(bf16[4,128,128]{2,1,0:T(8,128)(2,1)S(1)} %pad_maximum_fusion.refs_0_), channel_id=1, source_target_pairs={{0,16},{8,24},{16,0},{24,8},{32,48},{40,56},{48,32},{56,40},{64,80... | collective-permute-start | bytes 393224 | tf_op jit(solution)/shard_map/ppermute | solution.py:233
  28.1 9.9 %all-to-all-start.1 = ((f32[8,32,128]{2,1,0:T(8,128)}), f32[8,32,128]{2,1,0:T(8,128)S(1)}, u32[]{:S(2)}, u32[]{:S(2)}) async-start(f32[8,32,128]{2,1,0:T(8,128)} %bitcast), calls=%async_computation.1 | async-start | bytes 262144 | tf_op jit(solution)/shard_map/all_to_all | solution.py:256
  31.4 1.4 %collective-permute-start.6 = (bf16[4,128,128]{2,1,0:T(8,128)(2,1)S(1)}, bf16[4,128,128]{2,1,0:T(8,128)(2,1)S(1)}, u32[]{:S(2)}, u32[]{:S(2)}) collective-permute-start(bf16[4,128,128]{2,1,0:T(8,128)(2,1)S(1)} %pad_maximum_fusion.refs_0_), channel_id=1, source_target_pairs={{0,8},{8,0},{16,24},{24,16},{32,40},{40,32},{48,56},{56,48},{64,72... | collective-permute-start | bytes 393224 | tf_op jit(solution)/shard_map/ppermute | solution.py:233
  31.5 1.5 %collective-permute-start.9 = (bf16[4,128,128]{2,1,0:T(8,128)(2,1)S(1)}, bf16[4,128,128]{2,1,0:T(8,128)(2,1)S(1)}, u32[]{:S(2)}, u32[]{:S(2)}) collective-permute-start(bf16[4,128,128]{2,1,0:T(8,128)(2,1)S(1)} %collective-permute-done.5.refs_3_), channel_id=1, source_target_pairs={{0,8},{8,0},{16,24},{24,16},{32,40},{40,32},{48,56},{56,48},{64,72... | collective-permute-start | bytes 393224 | tf_op jit(solution)/shard_map/ppermute | solution.py:233
  32.0 1.3 %collective-permute-start.8 = (bf16[4,128,128]{2,1,0:T(8,128)(2,1)S(1)}, bf16[4,128,128]{2,1,0:T(8,128)(2,1)S(1)}, u32[]{:S(2)}, u32[]{:S(2)}) collective-permute-start(bf16[4,128,128]{2,1,0:T(8,128)(2,1)S(1)} %collective-permute-done.4.refs_2_), channel_id=1, source_target_pairs={{0,8},{8,0},{16,24},{24,16},{32,40},{40,32},{48,56},{56,48},{64,72... | collective-permute-start | bytes 393224 | tf_op jit(solution)/shard_map/ppermute | solution.py:233
  32.2 1.4 %collective-permute-start.7 = (bf16[4,128,128]{2,1,0:T(8,128)(2,1)S(1)}, bf16[4,128,128]{2,1,0:T(8,128)(2,1)S(1)}, u32[]{:S(2)}, u32[]{:S(2)}) collective-permute-start(bf16[4,128,128]{2,1,0:T(8,128)(2,1)S(1)} %collective-permute-done.3.refs_1_), channel_id=1, source_target_pairs={{0,8},{8,0},{16,24},{24,16},{32,40},{40,32},{48,56},{56,48},{64,72... | collective-permute-start | bytes 393224 | tf_op jit(solution)/shard_map/ppermute | solution.py:233

commit v6 on v5

--- a/solution.py
+++ b/solution.py
@@ -135,9 +135,12 @@
     total = total + own_ref[...]
     picks = total.shape[1] // 2
     half = picks // 2
-    outer = lax.dot_general(
-        total, total, (((0,), (0,)), ((), ())), precision=lax.Precision.HIGHEST, preferred_element_type=F32
-    )
+    high = total.astype(BF16)
+    low = (total - high.astype(F32)).astype(BF16)
+    across = (((0,), (0,)), ((), ()))
+    outer = lax.dot_general(high, high, across, preferred_element_type=F32)
+    outer = outer + lax.dot_general(high, low, across, preferred_element_type=F32)
+    outer = outer + lax.dot_general(low, high, across, preferred_element_type=F32)
     sketch = scale * jnp.concatenate(
         [outer[picks : picks + half, :picks], outer[picks + half :, :picks]], axis=1
     )

time: 39.2 us -> 39.2 us (level)
  no operation moved by 1% of the time
where the time goes in v6:
time: 39.2 us; the launch traced here: 38.9 us
  starting transfers between devices  22.8 us (58%)
  waiting for transfers between devices  10.1 us (26%)
  Pallas kernels  5.89 us (15%)
    ppermute x10, starting transfers between devices, swap(): return lax.ppermute(value, 'dp', pairs)  14.8 us
    all_to_all x1, starting transfers between devices, on_device(): mine = lax.all_to_all(term, 'tensor', 0, 0, tiled=True)  4.58 us
    all_to_all x1, waiting for transfers between devices, on_device(): sketches = lax.all_to_all(spread, 'tensor', 0, 0, tiled=True)  4.38 us
    pallas_call x1, Pallas kernels, terms(): pl.pallas_call(functools.partial(terms_kernel, parts), out_shape=(jax.Sha...  3.8 us
    all_to_all x1, waiting for transfers between devices, on_device(): mine = lax.all_to_all(term, 'tensor', 0, 0, tiled=True)  3.73 us
    all_to_all x1, starting transfers between devices, on_device(): sketches = lax.all_to_all(spread, 'tensor', 0, 0, tiled=True)  3.37 us
    ppermute x10, waiting for transfers between devices, swap(): return lax.ppermute(value, 'dp', pairs)  1.99 us
    pallas_call x1, Pallas kernels, sketch(): pl.pallas_call(functools.partial(sketch_kernel, scale), out_shape=jax.Sha...  1.07 us
  transfers between devices with their start and end apart: 12, of which 7 were waited for; matrix products, arithmetic and copies ran while one was open for 0% of the time, Pallas kernels for 13%

profile of v6, /device:TPU:2, one launch (start us, length us, event | category | flops | bytes accessed | tf_op | source)
XLA Modules:
  0.0 38.9 jit_solution(3804639060635950422)
XLA Ops:
  0.0 0.0 copy-start.3
  0.0 0.0 copy-start.2
  0.0 7.3 %collective-permute-start.2 = (bf16[128,128]{1,0:T(8,128)(2,1)}, bf16[128,128]{1,0:T(8,128)(2,1)S(1)}, u32[]{:S(2)}, u32[]{:S(2)}) collective-permute-start(bf16[128,128]{1,0:T(8,128)(2,1)} %param.13), channel_id=1, source_target_pairs={{0,128},{8,136},{16,144},{24,152},{32,160},{40,168},{48,176},{56,1... | collective-permute-start | bytes 98312 | tf_op jit(solution)/shard_map/ppermute | solution.py:236
  7.4 0.1 collective-permute-start.1
  7.5 1.6 %collective-permute-start = (bf16[128,128]{1,0:T(8,128)(2,1)S(1)}, bf16[128,128]{1,0:T(8,128)(2,1)S(1)}, u32[]{:S(2)}, u32[]{:S(2)}) collective-permute-start(bf16[128,128]{1,0:T(8,128)(2,1)S(1)} %copy-done.6), channel_id=1, source_target_pairs={{0,64},{8,72},{16,80},{24,88},{32,96},{40,104},{48,112},{56,120},{... | collective-permute-start | bytes 98312 | tf_op jit(solution)/shard_map/ppermute | solution.py:236
  9.0 0.0 copy-done.2
  9.0 0.0 copy-done.1
  9.0 0.0 copy-done
  9.0 3.8 %terms.1 = (bf16[8,256,128]{2,1,0:T(8,128)(2,1)}, f32[256,128]{1,0:T(8,128)S(1)}) custom-call(bf16[8,256,1792]{2,1,0:T(8,128)(2,1)S(1)} %copy-done, bf16[8,256,512]{2,1,0:T(8,128)(2,1)S(1)} %copy-done.1, s32[1792]{0:T(1024)S(1)} %copy-done.2, s32[512]{0:T(512)S(1)} %copy-done.3, s32[64]{0:T(128)S(1)} %copy-done.4, s32[64]{0:T(128)S(1)} %copy-done.5, ...), custom_call_target="tpu_custom_call" | custom-call | flops 1207959552 | bytes 9437184 | tf_op jit(solution)/shard_map/terms/pallas_call | solution.py:105
  12.9 0.0 collective-permute-done.2
  12.9 1.0 %collective-permute-done.1 = bf16[128,128]{1,0:T(8,128)(2,1)S(1)} collective-permute-done((bf16[128,128]{1,0:T(8,128)(2,1)S(1)}, bf16[128,128]{1,0:T(8,128)(2,1)S(1)}, u32[]{:S(2)}, u32[]{:S(2)}) %collective-permute-start.1) | collective-permute-done | bytes 32800 | tf_op jit(solution)/shard_map/ppermute | solution.py:236
  13.8 0.0 collective-permute-done
  13.8 4.6 %all-to-all-start = ((bf16[8,256,128]{2,1,0:T(8,128)(2,1)}), bf16[8,256,128]{2,1,0:T(8,128)(2,1)S(1)}, u32[]{:S(2)}, u32[]{:S(2)}) async-start(bf16[8,256,128]{2,1,0:T(8,128)(2,1)} %get-tuple-element.23), calls=%async_computation | async-start | bytes 1048576 | tf_op jit(solution)/shard_map/all_to_all | solution.py:256
  18.4 2.2 %collective-permute-start.5 = (bf16[4,128,128]{2,1,0:T(8,128)(2,1)S(1)}, bf16[4,128,128]{2,1,0:T(8,128)(2,1)S(1)}, u32[]{:S(2)}, u32[]{:S(2)}) collective-permute-start(bf16[4,128,128]{2,1,0:T(8,128)(2,1)S(1)} %pad_maximum_fusion.refs_0_), channel_id=1, source_target_pairs={{0,32},{8,40},{16,48},{24,56},{32,0},{40,8},{48,16},{56,24},{64,96... | collective-permute-start | bytes 393224 | tf_op jit(solution)/shard_map/ppermute | solution.py:236
  20.6 0.0 collective-permute-start.4
  20.6 2.6 %collective-permute-start.3 = (bf16[4,128,128]{2,1,0:T(8,128)(2,1)S(1)}, bf16[4,128,128]{2,1,0:T(8,128)(2,1)S(1)}, u32[]{:S(2)}, u32[]{:S(2)}) collective-permute-start(bf16[4,128,128]{2,1,0:T(8,128)(2,1)S(1)} %pad_maximum_fusion.refs_0_), channel_id=1, source_target_pairs={{0,16},{8,24},{16,0},{24,8},{32,48},{40,56},{48,32},{56,40},{64,80... | collective-permute-start | bytes 393224 | tf_op jit(solution)/shard_map/ppermute | solution.py:236
  23.2 3.7 %all-to-all-done.parts_ref = bf16[8,256,128]{2,1,0:T(8,128)(2,1)S(1)} async-done(((bf16[8,256,128]{2,1,0:T(8,128)(2,1)}), bf16[8,256,128]{2,1,0:T(8,128)(2,1)S(1)}, u32[]{:S(2)}, u32[]{:S(2)}) %all-to-all-start) | async-done | bytes 524320 | tf_op jit(solution)/shard_map/all_to_all | solution.py:256
  26.9 1.1 %sketch.1 = f32[256,128]{1,0:T(8,128)} custom-call(bf16[8,256,128]{2,1,0:T(8,128)(2,1)S(1)} %all-to-all-done.parts_ref, f32[256,128]{1,0:T(8,128)S(1)} %get-tuple-element.24.own_ref), custom_call_target="tpu_custom_call" | custom-call | flops 50331648 | bytes 524288 | tf_op jit(solution)/shard_map/sketch/pallas_call | solution.py:154
  28.0 3.4 %all-to-all-start.1 = ((f32[8,32,128]{2,1,0:T(8,128)}), f32[8,32,128]{2,1,0:T(8,128)S(1)}, u32[]{:S(2)}, u32[]{:S(2)}) async-start(f32[8,32,128]{2,1,0:T(8,128)} %bitcast), calls=%async_computation.1 | async-start | bytes 262144 | tf_op jit(solution)/shard_map/all_to_all | solution.py:259
  31.4 0.1 collective-permute-start.6
  31.5 0.0 collective-permute-done.5.refs_3_
  31.5 0.5 %collective-permute-start.9 = (bf16[4,128,128]{2,1,0:T(8,128)(2,1)S(1)}, bf16[4,128,128]{2,1,0:T(8,128)(2,1)S(1)}, u32[]{:S(2)}, u32[]{:S(2)}) collective-permute-start(bf16[4,128,128]{2,1,0:T(8,128)(2,1)S(1)} %collective-permute-done.5.refs_3_), channel_id=1, source_target_pairs={{0,8},{8,0},{16,24},{24,16},{32,40},{40,32},{48,56},{56,48},{64,72... | collective-permute-start | bytes 393224 | tf_op jit(solution)/shard_map/ppermute | solution.py:236
  32.0 0.0 collective-permute-done.4.refs_2_
  32.0 0.1 collective-permute-start.8
  32.1 0.0 collective-permute-done.3.refs_1_
  32.1 0.4 %collective-permute-start.7 = (bf16[4,128,128]{2,1,0:T(8,128)(2,1)S(1)}, bf16[4,128,128]{2,1,0:T(8,128)(2,1)S(1)}, u32[]{:S(2)}, u32[]{:S(2)}) collective-permute-start(bf16[4,128,128]{2,1,0:T(8,128)(2,1)S(1)} %collective-permute-done.3.refs_1_), channel_id=1, source_target_pairs={{0,8},{8,0},{16,24},{24,16},{32,40},{40,32},{48,56},{56,48},{64,72... | collective-permute-start | bytes 393224 | tf_op jit(solution)/shard_map/ppermute | solution.py:236
  32.5 0.3 collective-permute-done.6.refs_4_
  32.8 0.2 collective-permute-done.9.refs_7_
  33.0 0.3 collective-permute-done.8.refs_6_
  33.3 0.2 collective-permute-done.7.refs_5_
  33.5 4.4 %all-to-all-done.1 = f32[8,32,128]{2,1,0:T(8,128)S(1)} async-done(((f32[8,32,128]{2,1,0:T(8,128)}), f32[8,32,128]{2,1,0:T(8,128)S(1)}, u32[]{:S(2)}, u32[]{:S(2)}) %all-to-all-start.1) | async-done | bytes 131104 | tf_op jit(solution)/shard_map/all_to_all | solution.py:259
  37.9 1.0 %scores.1 = f32[8,128]{1,0:T(8,128)} custom-call(f32[256,128]{1,0:T(8,128)S(1)} %bitcast.6, bf16[4,128,128]{2,1,0:T(8,128)(2,1)S(1)} %pad_maximum_fusion.refs_0_, bf16[4,128,128]{2,1,0:T(8,128)(2,1)S(1)} %collective-permute-done.3.refs_1_, bf16[4,128,128]{2,1,0:T(8,128)(2,1)S(1)} %collective-permute-done.4.refs_2_, ...), custom_call_target="tpu_custom_call" | custom-call | tf_op jit(solution)/shard_map/scores/pallas_call | solution.py:193
  (11 shorter events, 0.1 us)
Async XLA Ops:
  0.0 7.3 %copy-start.6 = (bf16[128,128]{1,0:T(8,128)(2,1)S(1)}, bf16[128,128]{1,0:T(8,128)(2,1)}, u32[]{:S(2)}) copy-start(bf16[128,128]{1,0:T(8,128)(2,1)} %param.13) | copy-start | bytes 98308
  0.0 9.0 %copy-start.5 = (s32[64]{0:T(128)S(1)}, s32[64]{0:T(128)}, u32[]{:S(2)}) copy-start(s32[64]{0:T(128)} %pick_out.1) | copy-start | bytes 772
  0.0 9.0 %copy-start.4 = (s32[64]{0:T(128)S(1)}, s32[64]{0:T(128)}, u32[]{:S(2)}) copy-start(s32[64]{0:T(128)} %pick_in.1) | copy-start | bytes 772
  0.0 9.0 %copy-start.3 = (s32[512]{0:T(512)S(1)}, s32[512]{0:T(512)}, u32[]{:S(2)}) copy-start(s32[512]{0:T(512)} %sign_out.1) | copy-start | bytes 6148
  0.0 9.0 %copy-start.2 = (s32[1792]{0:T(1024)S(1)}, s32[1792]{0:T(1024)}, u32[]{:S(2)}) copy-start(s32[1792]{0:T(1024)} %sign_in.1) | copy-start | bytes 21508
  0.0 9.0 %copy-start.1 = (bf16[8,256,512]{2,1,0:T(8,128)(2,1)S(1)}, bf16[8,256,512]{2,1,0:T(8,128)(2,1)}, u32[]{:S(2)}) copy-start(bf16[8,256,512]{2,1,0:T(8,128)(2,1)} %grad.1) | copy-start | bytes 6291460
  0.0 9.0 %copy-start = (bf16[8,256,1792]{2,1,0:T(8,128)(2,1)S(1)}, bf16[8,256,1792]{2,1,0:T(8,128)(2,1)}, u32[]{:S(2)}) copy-start(bf16[8,256,1792]{2,1,0:T(8,128)(2,1)} %act.1) | copy-start | bytes 22020100
  0.0 12.8 %collective-permute-start.2 = (bf16[128,128]{1,0:T(8,128)(2,1)}, bf16[128,128]{1,0:T(8,128)(2,1)S(1)}, u32[]{:S(2)}, u32[]{:S(2)}) collective-permute-start(bf16[128,128]{1,0:T(8,128)(2,1)} %param.13), channel_id=1, source_target_pairs={{0,128},{8,136},{16,144},{24,152},{32,160},{40,168},{48,176},{56,1... | collective-permute-start | bytes 98312 | tf_op jit(solution)/shard_map/ppermute | solution.py:236
  7.4 6.5 %collective-permute-start.1 = (bf16[128,128]{1,0:T(8,128)(2,1)S(1)}, bf16[128,128]{1,0:T(8,128)(2,1)S(1)}, u32[]{:S(2)}, u32[]{:S(2)}) collective-permute-start(bf16[128,128]{1,0:T(8,128)(2,1)S(1)} %copy-done.6), channel_id=1, source_target_pairs={{0,192},{8,200},{16,208},{24,216},{32,224},{40,232},{48,240},{56,2... | collective-permute-start | bytes 98312 | tf_op jit(solution)/shard_map/ppermute | solution.py:236
  7.5 6.4 %collective-permute-start = (bf16[128,128]{1,0:T(8,128)(2,1)S(1)}, bf16[128,128]{1,0:T(8,128)(2,1)S(1)}, u32[]{:S(2)}, u32[]{:S(2)}) collective-permute-start(bf16[128,128]{1,0:T(8,128)(2,1)S(1)} %copy-done.6), channel_id=1, source_target_pairs={{0,64},{8,72},{16,80},{24,88},{32,96},{40,104},{48,112},{56,120},{... | collective-permute-start | bytes 98312 | tf_op jit(solution)/shard_map/ppermute | solution.py:236
  13.8 13.1 %all-to-all-start = ((bf16[8,256,128]{2,1,0:T(8,128)(2,1)}), bf16[8,256,128]{2,1,0:T(8,128)(2,1)S(1)}, u32[]{:S(2)}, u32[]{:S(2)}) async-start(bf16[8,256,128]{2,1,0:T(8,128)(2,1)} %get-tuple-element.23), calls=%async_computation | async-start | bytes 1048576 | tf_op jit(solution)/shard_map/all_to_all | solution.py:256
  18.4 13.1 %collective-permute-start.5 = (bf16[4,128,128]{2,1,0:T(8,128)(2,1)S(1)}, bf16[4,128,128]{2,1,0:T(8,128)(2,1)S(1)}, u32[]{:S(2)}, u32[]{:S(2)}) collective-permute-start(bf16[4,128,128]{2,1,0:T(8,128)(2,1)S(1)} %pad_maximum_fusion.refs_0_), channel_id=1, source_target_pairs={{0,32},{8,40},{16,48},{24,56},{32,0},{40,8},{48,16},{56,24},{64,96... | collective-permute-start | bytes 393224 | tf_op jit(solution)/shard_map/ppermute | solution.py:236
  20.6 11.4 %collective-permute-start.4 = (bf16[4,128,128]{2,1,0:T(8,128)(2,1)S(1)}, bf16[4,128,128]{2,1,0:T(8,128)(2,1)S(1)}, u32[]{:S(2)}, u32[]{:S(2)}) collective-permute-start(bf16[4,128,128]{2,1,0:T(8,128)(2,1)S(1)} %pad_maximum_fusion.refs_0_), channel_id=1, source_target_pairs={{0,48},{8,56},{16,32},{24,40},{32,16},{40,24},{48,0},{56,8},{64,11... | collective-permute-start | bytes 393224 | tf_op jit(solution)/shard_map/ppermute | solution.py:236
  20.6 11.5 %collective-permute-start.3 = (bf16[4,128,128]{2,1,0:T(8,128)(2,1)S(1)}, bf16[4,128,128]{2,1,0:T(8,128)(2,1)S(1)}, u32[]{:S(2)}, u32[]{:S(2)}) collective-permute-start(bf16[4,128,128]{2,1,0:T(8,128)(2,1)S(1)} %pad_maximum_fusion.refs_0_), channel_id=1, source_target_pairs={{0,16},{8,24},{16,0},{24,8},{32,48},{40,56},{48,32},{56,40},{64,80... | collective-permute-start | bytes 393224 | tf_op jit(solution)/shard_map/ppermute | solution.py:236
  28.0 9.9 %all-to-all-start.1 = ((f32[8,32,128]{2,1,0:T(8,128)}), f32[8,32,128]{2,1,0:T(8,128)S(1)}, u32[]{:S(2)}, u32[]{:S(2)}) async-start(f32[8,32,128]{2,1,0:T(8,128)} %bitcast), calls=%async_computation.1 | async-start | bytes 262144 | tf_op jit(solution)/shard_map/all_to_all | solution.py:259
  31.4 1.4 %collective-permute-start.6 = (bf16[4,128,128]{2,1,0:T(8,128)(2,1)S(1)}, bf16[4,128,128]{2,1,0:T(8,128)(2,1)S(1)}, u32[]{:S(2)}, u32[]{:S(2)}) collective-permute-start(bf16[4,128,128]{2,1,0:T(8,128)(2,1)S(1)} %pad_maximum_fusion.refs_0_), channel_id=1, source_target_pairs={{0,8},{8,0},{16,24},{24,16},{32,40},{40,32},{48,56},{56,48},{64,72... | collective-permute-start | bytes 393224 | tf_op jit(solution)/shard_map/ppermute | solution.py:236
  31.5 1.5 %collective-permute-start.9 = (bf16[4,128,128]{2,1,0:T(8,128)(2,1)S(1)}, bf16[4,128,128]{2,1,0:T(8,128)(2,1)S(1)}, u32[]{:S(2)}, u32[]{:S(2)}) collective-permute-start(bf16[4,128,128]{2,1,0:T(8,128)(2,1)S(1)} %collective-permute-done.5.refs_3_), channel_id=1, source_target_pairs={{0,8},{8,0},{16,24},{24,16},{32,40},{40,32},{48,56},{56,48},{64,72... | collective-permute-start | bytes 393224 | tf_op jit(solution)/shard_map/ppermute | solution.py:236
  32.0 1.3 %collective-permute-start.8 = (bf16[4,128,128]{2,1,0:T(8,128)(2,1)S(1)}, bf16[4,128,128]{2,1,0:T(8,128)(2,1)S(1)}, u32[]{:S(2)}, u32[]{:S(2)}) collective-permute-start(bf16[4,128,128]{2,1,0:T(8,128)(2,1)S(1)} %collective-permute-done.4.refs_2_), channel_id=1, source_target_pairs={{0,8},{8,0},{16,24},{24,16},{32,40},{40,32},{48,56},{56,48},{64,72... | collective-permute-start | bytes 393224 | tf_op jit(solution)/shard_map/ppermute | solution.py:236
  32.1 1.4 %collective-permute-start.7 = (bf16[4,128,128]{2,1,0:T(8,128)(2,1)S(1)}, bf16[4,128,128]{2,1,0:T(8,128)(2,1)S(1)}, u32[]{:S(2)}, u32[]{:S(2)}) collective-permute-start(bf16[4,128,128]{2,1,0:T(8,128)(2,1)S(1)} %collective-permute-done.3.refs_1_), channel_id=1, source_target_pairs={{0,8},{8,0},{16,24},{24,16},{32,40},{40,32},{48,56},{56,48},{64,72... | collective-permute-start | bytes 393224 | tf_op jit(solution)/shard_map/ppermute | solution.py:236
